TPU v7x, 32 devices: a whole 2x2x4 slice. The times are simulated.
32 devices in a mesh: tile: 16 (over z, y, x), head: 2 (over core).
Axes of the slice: x: 2, y: 2, z: 4, core: 2. Of those that a mesh axis runs over, the one named last changes fastest.
Arguments:
- queries: bfloat16 [4096, 1024], P('tile', 'head'), may hold values from -6 to 6
- keys: bfloat16 [4096, 1024], P('tile', 'head'), may hold values from -6 to 6
- values: bfloat16 [4096, 1024], P('tile', 'head'), may hold values from -6 to 6
- grad_output: bfloat16 [4096, 1024], P('tile', 'head'), may hold values from -6 to 6
- out_weight: bfloat16 [1024, 1024], P(None, 'head'), may hold values from -0.1875 to 0.1875
- rotations: int32 [16, 4], P('tile'), may hold values from 0 to 3, as said below
Outputs:
- grad_queries: bfloat16 [4096, 1024], P('tile', 'head')
- grad_keys: bfloat16 [4096, 1024], P('tile', 'head')
- grad_values: bfloat16 [4096, 1024], P('tile', 'head')
- grad_out_weight: float32 [1024, 1024], P('tile', 'head')
Inputs may be any that keep to these rules, and one draw needn't show every extreme that they name: The tiles form 4 rows of 4 in row-major order, grouped into faces of max(1, 2) whole columns; rotations[t, s] is 0 unless side s of tile t crosses a seam, that is an east or west side between two faces or a north or south side between the last and the first row. Across a seam the two facing sides hold r and (4 - r) mod 4 with r equal to 1 or 3.
All inputs are finite; a program needn't handle non-finite values.
Results may differ from a plain program's by a relative error of at most 0.012.
Values may be sent and summed in bfloat16 or wider, within the bound.
No kernel may reach another device: no remote copies, remote signals or barrier semaphores. Data moves between devices by JAX's collectives and lax.ppermute only.
A program may use at most 64 MiB of HBM per device.

v0:
```python
import functools
import math

import jax
import jax.numpy as jnp
from jax import lax
from jax.experimental import pallas as pl
from jax.experimental.pallas import tpu as pltpu
from jax.sharding import PartitionSpec as P

HEAD_DIM = 64
RADIUS = 6
SIDE = 16
CELLS = SIDE * SIDE
STRIP = RADIUS * SIDE
NEAR = 4
LANES = 128
PAIR = 2 * HEAD_DIM
VMEM_LIMIT = 32 * 1024 * 1024
NT = (((1,), (1,)), ((), ()))


def mm(a, b):
    return jnp.dot(a, b, preferred_element_type=jnp.float32)


def mm_nt(a, b):
    return lax.dot_general(a, b, NT, preferred_element_type=jnp.float32)


def strip_token(side_index, rotation, cell):
    turn = lax.rem(side_index + 6 - rotation, 4)
    depth = cell >> 4
    along = cell & (SIDE - 1)
    far = SIDE - 1 - along
    near_rim = RADIUS - 1 - depth
    far_rim = SIDE - RADIUS + depth
    row = jnp.where(turn == 0, far_rim, jnp.where(turn == 1, along, jnp.where(turn == 2, near_rim, far)))
    col = jnp.where(turn == 0, along, jnp.where(turn == 1, near_rim, jnp.where(turn == 2, far, far_rim)))
    return row * SIDE + col


def slot_side(slot, columns):
    tile = lax.axis_index("tile")
    if slot < 2:
        return jnp.where((tile + slot) & 1 == 0, 1, 3)
    return jnp.where((lax.div(tile, columns) + slot) & 1 == 0, 2, 0)


def partner(tile, tile_count, slot):
    columns = tile_count // 4
    if slot < 2:
        return (tile + (1 if (tile + slot) % 2 == 0 else -1)) % tile_count
    return (tile + (columns if (tile // columns + slot) % 2 == 0 else -columns)) % tile_count


def pick_kernel(columns, rotations_ref, keys_ref, values_ref, *out_refs):
    cell = lax.broadcasted_iota(jnp.int32, (STRIP, CELLS), 0)
    token = lax.broadcasted_iota(jnp.int32, (STRIP, CELLS), 1)
    for slot, out_ref in enumerate(out_refs):
        side = slot_side(slot, columns)
        wanted = strip_token(side, rotations_ref[0, side], cell)
        chosen = jnp.where(token == wanted, 1.0, 0.0).astype(jnp.bfloat16)
        out_ref[0] = mm(chosen, keys_ref[...]).astype(jnp.bfloat16)
        out_ref[1] = mm(chosen, values_ref[...]).astype(jnp.bfloat16)


def weight_kernel(scale, *refs):
    total = refs[0][0].astype(jnp.float32)
    for ref in refs[1:-1]:
        total += ref[0].astype(jnp.float32)
    refs[-1][...] = total * scale


def partial_kernel(attention_ref, arrived_ref, turned_ref, turned_arrived_ref, unused_ref, kept_ref, sent_ref):
    for index, out_ref in enumerate((kept_ref, sent_ref)):
        total = None
        for turned_part, attention_part in ((turned_ref, attention_ref), (turned_arrived_ref, arrived_ref)):
            turned = turned_part[index]
            turned = turned.reshape(turned.shape[0] * turned.shape[1], turned.shape[2])
            term = mm(turned, attention_part[...])
            total = term if total is None else total + term
        out_ref[...] = total.astype(out_ref.dtype).reshape(out_ref.shape)


def sum_kernel(count, *refs):
    terms, outs = refs[:count], refs[count + 3 :]
    for q in range(terms[0].shape[0]):
        total = terms[0][q].astype(jnp.float32)
        for ref in terms[1:]:
            total += ref[q].astype(jnp.float32)
        outs[q % len(outs)][q // len(outs)] = total.astype(jnp.bfloat16)


def rim_token(side_index, place):
    depth = place >> 4
    along = place & (SIDE - 1)
    last = SIDE - 1
    north, east, south = side_index == 0, side_index == 1, side_index == 2
    row = jnp.where(north, depth, jnp.where(east, along, jnp.where(south, last - depth, last - along)))
    col = jnp.where(north, along, jnp.where(east, last - depth, jnp.where(south, last - along, depth)))
    return row * SIDE + col


def cotangent_kernel(heads, *refs):
    blocks, out_weight_ref, outs = refs[:heads], refs[heads], refs[heads + 1 :]
    dout_ref, dout_turned_ref, turned_ref, turned_sent_ref = outs
    head = lax.axis_index("head")
    axis = head & 1
    tile = lax.axis_index("tile")
    chunk = turned_ref.shape[2]
    width = blocks[0].shape[1]
    total = None
    for distance, block_ref in enumerate(blocks):
        owner = lax.rem(head + distance, heads)
        start = pl.multiple_of(owner * width, width)
        block = block_ref[...]
        term = mm(block, out_weight_ref[pl.ds(start, width), :])
        total = term if total is None else total + term
        turned = block.T
        first = owner * (width // chunk)
        for index in range(width // chunk):
            target = (first + index) ^ tile
            rows = turned[index * chunk : (index + 1) * chunk]
            for parity, out_ref in enumerate((turned_ref, turned_sent_ref)):

                @pl.when((target >> axis) & 1 == parity)
                def _():
                    out_ref[(target >> (1 - axis)) & 1, target >> 2] = rows

    dout = total.astype(jnp.bfloat16)
    dout_ref[...] = dout
    dout_turned_ref[...] = dout.T


def split(exact, count):
    parts = []
    for _ in range(count):
        part = exact.astype(jnp.bfloat16).astype(jnp.float32)
        parts.append(part)
        exact = exact - part
    return parts


PARTS = (3, 2, 2)
SIDE_ORDER = (3, 2, 1, 0)


def rim_kernel(query_ref, dout_ref, rows_ref, chosen_ref, unused_ref, *rim_refs):
    parts = [part for kind, count in enumerate(PARTS) for part in split(rows_ref[kind], count)]
    pairs = rows_ref.shape[1] // 2
    filler = jnp.zeros((16 - 2 * len(parts), CELLS), jnp.float32)
    rows = [
        jnp.concatenate([part[2 * pair : 2 * pair + 2] for part in parts] + [filler], axis=0) for pair in range(pairs)
    ]
    rows = jnp.concatenate(rows, axis=0).astype(jnp.bfloat16)
    for slot, rim_ref in enumerate(rim_refs):
        chosen = chosen_ref[slot]
        rim_ref[:STRIP] = mm(chosen[:STRIP], query_ref[...]).astype(jnp.bfloat16)
        rim_ref[STRIP : 2 * STRIP] = mm(chosen[:STRIP], dout_ref[...]).astype(jnp.bfloat16)
        spread = mm_nt(rows, chosen).astype(jnp.bfloat16)
        for pair in range(pairs):
            rim_ref[2 * STRIP :, pair * PAIR : (pair + 1) * PAIR] = spread[16 * pair : 16 * pair + 16]


def window(cell_row, cell_col, query):
    query_row = (query >> 4) + RADIUS
    query_col = (query & (SIDE - 1)) + RADIUS
    near = (jnp.abs(cell_row - query_row) <= RADIUS) & (jnp.abs(cell_col - query_col) <= RADIUS)
    return jnp.where(near, 0.0, -1e30)


def centre_bias(bias_ref):
    query = lax.broadcasted_iota(jnp.int32, (CELLS, CELLS), 1)
    cell = lax.broadcasted_iota(jnp.int32, (CELLS, CELLS), 0)
    bias_ref[...] = window((cell >> 4) + RADIUS, (cell & (SIDE - 1)) + RADIUS, query)


def strip_bias(kind, bias_ref):
    query = lax.broadcasted_iota(jnp.int32, (STRIP, CELLS), 1)
    cell = lax.broadcasted_iota(jnp.int32, (STRIP, CELLS), 0)
    depth = cell >> 4
    along = cell & (SIDE - 1)
    last = SIDE + 2 * RADIUS - 1
    if kind:
        first, second = (last - RADIUS - along, depth), (RADIUS + along, last - depth)
    else:
        first, second = (depth, RADIUS + along), (last - depth, last - RADIUS - along)
    in_first = first_half(query, kind)
    row = jnp.where(in_first, first[0], second[0])
    col = jnp.where(in_first, first[1], second[1])
    bias_ref[...] = window(row, col, query)


def first_half(query, kind):
    return (query & (SIDE - 1)) < SIDE // 2 if kind else query < CELLS // 2


def one_head(block, head):
    lane = lax.broadcasted_iota(jnp.int32, block.shape, 1)
    kept = (lane >= HEAD_DIM) if head else (lane < HEAD_DIM)
    return jnp.where(kept, block, jnp.zeros_like(block))


def halves(block, kind):
    kept = first_half(lax.broadcasted_iota(jnp.int32, block.shape, 0), kind)
    zero = jnp.zeros_like(block)
    return jnp.concatenate([jnp.where(kept, block, zero), jnp.where(kept, zero, block)], axis=1)


def by_half(stacked, kind):
    rows = stacked.shape[0] // 2
    kept = first_half(lax.broadcasted_iota(jnp.int32, (rows, CELLS), 1), kind)
    return jnp.where(kept, stacked[:rows], stacked[rows:])


def side_blocks(strips, part, kind, cols):
    tile = lax.axis_index("tile")
    second, first = strips
    straight = (tile if kind else lax.div(tile, lax.axis_size("tile") // 4)) & 1 == 0
    first, second = first[part, :, cols], second[part, :, cols]
    return jnp.where(straight, first, second), jnp.where(straight, second, first)


def side_cells(strips, part, kind, cols):
    return jnp.concatenate(side_blocks(strips, part, kind, cols), axis=1)


def halves(block, kind):
    kept = first_half(lax.broadcasted_iota(jnp.int32, block.shape, 0), kind)
    zero = jnp.zeros_like(block)
    return jnp.concatenate([jnp.where(kept, block, zero), jnp.where(kept, zero, block)], axis=1)


def by_half(stacked, kind):
    rows = stacked.shape[0] // 2
    kept = first_half(lax.broadcasted_iota(jnp.int32, (rows, CELLS), 1), kind)
    return jnp.where(kept, stacked[:rows], stacked[rows:])


def side_blocks(strips, part, kind, cols):
    tile = lax.axis_index("tile")
    second, first = strips
    straight = (tile if kind else lax.div(tile, lax.axis_size("tile") // 4)) & 1 == 0
    first, second = first[part, :, cols], second[part, :, cols]
    return jnp.where(straight, first, second), jnp.where(straight, second, first)


def side_cells(strips, part, kind, cols):
    return jnp.concatenate(side_blocks(strips, part, kind, cols), axis=1)


def side_products(cells, rows_head):
    return [mm_nt(cells[kind], halves(rows_head, kind)) for kind in range(2)]


def turned_sides(strips, part, kind, cols):
    return [block.T for block in side_blocks(strips, part, kind, cols)]


def pair_cols(pair):
    return pl.ds(pl.multiple_of(pair * PAIR, PAIR), PAIR)


def head_rows(turned, head):
    return turned[head * HEAD_DIM : (head + 1) * HEAD_DIM]


def over_side(turned, head, kind, sides):
    return by_half(mm(jnp.concatenate([head_rows(t, head) for t in turned], axis=0), sides), kind)


SCORE_SCALE = HEAD_DIM ** (-0.5)
LOG_SCALE = SCORE_SCALE * math.log2(math.e)


def lanes_of(head):
    return slice(head * CELLS, (head + 1) * CELLS)


def centre_kernel(
    query_ref, key_ref, value_ref, dout_ref,
    raw_ref, stats_ref, sums_ref, product_ref, query_out, key_out, bias_ref,
):
    centre_bias(bias_ref)

    def step(pair, carry):
        cols = pair_cols(pair)
        query, key, value, dout = (ref[:, cols] for ref in (query_ref, key_ref, value_ref, dout_ref))
        turned = value.T
        for head in range(2):
            lanes = lanes_of(head)
            scores = mm_nt(key, one_head(query, head)) + bias_ref[...]
            top = jnp.max(scores, axis=0, keepdims=True)
            raw = jnp.exp2((scores - top) * LOG_SCALE)
            raw_ref[pair, :, lanes] = raw
            stats_ref[pair, 0:1, lanes] = top
            stats_ref[pair, 1:2, lanes] = jnp.sum(raw, axis=0, keepdims=True)
            sums_ref[pair, :, lanes] = mm(head_rows(turned, head), raw.astype(jnp.bfloat16))
            product_ref[pair, :, lanes] = mm_nt(value, one_head(dout, head))
        query_out[:, cols] = query
        key_out[:, cols] = key
        return carry

    lax.fori_loop(0, raw_ref.shape[0], step, 0)


def column_kernel(
    columns, rotations_ref, first_ref, second_ref, query_ref, dout_ref,
    raw_ref, stats_ref, sums_ref, product_ref, row_bias_ref, rim_chosen_ref, chosen_ref, bias_ref,
):
    strips = (first_ref, second_ref)
    strip_bias(0, bias_ref)
    strip_bias(1, row_bias_ref)
    place = lax.broadcasted_iota(jnp.int32, (LANES, CELLS), 0)
    token = lax.broadcasted_iota(jnp.int32, (LANES, CELLS), 1)
    for slot in range(4):
        wanted = rim_token(slot_side(slot, columns), place)
        chosen = jnp.where((token == wanted) & (place < STRIP), 1.0, 0.0).astype(jnp.bfloat16)
        rim_chosen_ref[slot] = chosen
    place = lax.broadcasted_iota(jnp.int32, (CELLS, LANES), 1)
    token = lax.broadcasted_iota(jnp.int32, (CELLS, LANES), 0)
    for index, slot in enumerate(SIDE_ORDER):
        side = slot_side(slot, columns)
        wanted = jnp.where(place < STRIP, strip_token(side, rotations_ref[0, side], place), -1)
        chosen = jnp.where(token == wanted, 1.0, 0.0).astype(jnp.bfloat16)
        chosen_ref[:, index * LANES : (index + 1) * LANES] = chosen

    def step(pair, carry):
        cols = pair_cols(pair)
        keys = side_cells(strips, 0, 0, cols)
        values = side_cells(strips, 1, 0, cols)
        turned = turned_sides(strips, 1, 0, cols)
        for head in range(2):
            lanes = lanes_of(head)
            scores = mm_nt(keys, halves(one_head(query_ref[:, cols], head), 0)) + bias_ref[...]
            top = jnp.max(scores, axis=0, keepdims=True)
            raw = jnp.exp2((scores - top) * LOG_SCALE)
            raw_ref[pair, :, lanes] = raw
            stats_ref[pair, 0:1, lanes] = top
            stats_ref[pair, 1:2, lanes] = jnp.sum(raw, axis=0, keepdims=True)
            sums_ref[pair, :, lanes] = over_side(turned, head, 0, raw.astype(jnp.bfloat16))
            product_ref[pair, :, lanes] = mm_nt(values, halves(one_head(dout_ref[:, cols], head), 0))
        return carry

    lax.fori_loop(0, raw_ref.shape[0], step, 0)


def row_kernel(
    first_ref, second_ref, query_ref, dout_turned_ref, centre_stats_ref, centre_sums_ref, stats_ref, sums_ref, bias_ref,
    raw_ref, attention_ref, rows_ref, factors_ref,
):
    strips = (first_ref, second_ref)

    def step(pair, carry):
        cols = pair_cols(pair)
        keys = side_cells(strips, 0, 1, cols)
        turned = turned_sides(strips, 1, 1, cols)
        parts = []
        for head in range(2):
            lanes = lanes_of(head)
            scores = mm_nt(keys, halves(one_head(query_ref[:, cols], head), 1)) + bias_ref[...]
            tops = [ref[pair, 0:1, lanes] for ref in (centre_stats_ref, stats_ref)]
            top = jnp.maximum(jnp.max(scores, axis=0, keepdims=True), jnp.maximum(*tops))
            raw = jnp.exp2((scores - top) * LOG_SCALE)
            raw_ref[pair, :, lanes] = raw
            lifted = [jnp.exp2((t - top) * LOG_SCALE) for t in tops]
            total = jnp.sum(raw, axis=0, keepdims=True)
            total += lifted[0] * centre_stats_ref[pair, 1:2, lanes] + lifted[1] * stats_ref[pair, 1:2, lanes]
            inverse = 1.0 / total
            factors = [l * inverse for l in lifted]
            part = over_side(turned, head, 1, raw.astype(jnp.bfloat16)) * inverse
            part += factors[0] * centre_sums_ref[pair, :, lanes] + factors[1] * sums_ref[pair, :, lanes]
            parts.append(part)
            place = pl.ds(2 * pair + head, 1)
            features = pl.ds(pl.multiple_of((2 * pair + head) * HEAD_DIM, HEAD_DIM), HEAD_DIM)
            product = dout_turned_ref[features, :].astype(jnp.float32) * part
            rows_ref[0, place, :] = top
            rows_ref[1, place, :] = inverse
            rows_ref[2, place, :] = jnp.sum(product, axis=0, keepdims=True)
            factors_ref[0, place, :] = factors[0]
            factors_ref[1, place, :] = factors[1]
        attention_ref[:, cols] = jnp.concatenate(parts, axis=0).T.astype(jnp.bfloat16)
        return carry

    lax.fori_loop(0, raw_ref.shape[0], step, 0, unroll=True)


def backward_kernel(
    fourth_ref, third_ref, second_ref, first_ref, query_ref, key_ref, dout_ref, centre_raw_ref, column_raw_ref,
    row_raw_ref, centre_product_ref, column_product_ref, rows_ref, factors_ref, unused_ref,
    grad_query_ref, centre_ref,
):
    columns, rows = (third_ref, fourth_ref), (first_ref, second_ref)

    def step(pair, carry):
        cols = pair_cols(pair)
        query = query_ref[:, cols]
        dout = dout_ref[:, cols]
        turned_centre = key_ref[:, cols].T
        turned_columns = turned_sides(columns, 0, 0, cols)
        turned_rows = turned_sides(rows, 0, 1, cols)
        row_values = side_cells(rows, 1, 1, cols)
        parts = []
        centre_scores = []
        centre_weights = []
        for head in range(2):
            lanes = lanes_of(head)
            place = pl.ds(2 * pair + head, 1)
            delta = rows_ref[2, place, :]
            row_product = mm_nt(row_values, halves(one_head(dout, head), 1))

            def dscore(weights, product):
                return (weights * (product - delta)).astype(jnp.bfloat16)

            weights = centre_raw_ref[pair, :, lanes] * factors_ref[0, place, :]
            centre_weights.append(weights.astype(jnp.bfloat16))
            centre_scores.append(dscore(weights, centre_product_ref[pair, :, lanes]))
            column_weights = column_raw_ref[pair, :, lanes] * factors_ref[1, place, :]
            column_score = dscore(column_weights, column_product_ref[pair, :, lanes])
            row_score = dscore(row_raw_ref[pair, :, lanes] * rows_ref[1, place, :], row_product)
            part = mm(head_rows(turned_centre, head), centre_scores[-1])
            part += over_side(turned_columns, head, 0, column_score) + over_side(turned_rows, head, 1, row_score)
            parts.append(part)
        grad_query = jnp.concatenate(parts, axis=0).T * SCORE_SCALE
        grad_query_ref[:, cols] = grad_query.astype(jnp.bfloat16)
        grad_key, grad_value = joint_mm(
            jnp.concatenate(centre_scores, axis=1),
            jnp.concatenate(centre_weights, axis=1),
            both_heads(query),
            both_heads(dout),
        )
        centre_ref[0, :, cols] = grad_key * SCORE_SCALE
        centre_ref[1, :, cols] = grad_value
        return carry

    lax.fori_loop(0, centre_raw_ref.shape[0], step, 0)


def joint_mm(first, second, first_rows, second_rows):
    rows = first.shape[0]
    product = mm(jnp.concatenate([first, second], axis=0), jnp.concatenate([first_rows, second_rows], axis=1))
    return product[:rows, :PAIR], product[rows:, PAIR:]


def both_heads(block):
    return jnp.concatenate([one_head(block, head) for head in range(2)], axis=0)


def padded(block):
    return jnp.concatenate([block, jnp.zeros((LANES - block.shape[0], block.shape[1]), block.dtype)], axis=0)


def statistics(rows):
    first = 0
    for count in PARTS:
        heads = []
        for head in range(2):
            parts = [rows[2 * index + head : 2 * index + head + 1] for index in range(first, first + count)]
            heads.append(functools.reduce(jnp.add, parts))
        first += count
        yield jnp.concatenate(heads, axis=1)


def side_kernel(centre_ref, chosen_ref, *refs):
    picked, rims = refs[:4], refs[4:8]
    keys_ref, values_ref, bias_ref, keys_done, values_done, sems = refs[8:]
    cell = lax.broadcasted_iota(jnp.int32, (STRIP, LANES), 0)
    query = lax.broadcasted_iota(jnp.int32, (STRIP, LANES), 1)
    near = jnp.abs((cell & (SIDE - 1)) - (query & (SIDE - 1))) <= RADIUS
    near = near & ((cell >> 4) >= (query >> 4)) & (query < STRIP)
    bias_ref[...] = jnp.where(near, 0.0, -1e30)
    copies = []
    for pair in range(keys_ref.shape[1] // PAIR):
        cols = slice(pair * PAIR, (pair + 1) * PAIR)
        grads = []
        bias = jnp.concatenate([bias_ref[...]] * 2, axis=1)
        for picked_ref, rim_ref in zip(picked, rims):
            query = both_heads(padded(rim_ref[:STRIP, cols]))
            dout = both_heads(padded(rim_ref[STRIP : 2 * STRIP, cols]))
            top, inverse, delta = statistics(rim_ref[2 * STRIP :, cols].astype(jnp.float32))
            scores = mm_nt(picked_ref[0, :, cols], query) + bias
            weights = jnp.exp2((scores - top) * LOG_SCALE) * inverse
            product = mm_nt(picked_ref[1, :, cols], dout)
            dscore = (weights * (product - delta)).astype(jnp.bfloat16)
            grad = jnp.concatenate([mm(dscore, query) * SCORE_SCALE, mm(weights.astype(jnp.bfloat16), dout)], axis=1)
            grads.append(padded(grad.astype(jnp.bfloat16)))
        total = mm(chosen_ref[...], jnp.concatenate(grads, axis=0))
        keys_done[:, cols] = (centre_ref[0, :, cols] + total[:, :PAIR]).astype(jnp.bfloat16)
        values_done[:, cols] = (centre_ref[1, :, cols] + total[:, PAIR:]).astype(jnp.bfloat16)
        for index, (done, out_ref) in enumerate(((keys_done, keys_ref), (values_done, values_ref))):
            copy = pltpu.make_async_copy(done.at[:, cols], out_ref.at[:, cols], sems.at[2 * pair + index])
            copy.start()
            copies.append(copy)
    for copy in copies:
        copy.wait()


def call(kernel, name, out_shape, operands, scratch=(), smem=0, unused=0, gflop=0.1, out_space=pltpu.VMEM):
    specs = [pl.BlockSpec(memory_space=pltpu.SMEM)] * smem
    specs += [pl.BlockSpec(memory_space=pltpu.VMEM)] * (len(operands) - smem - unused)
    specs += [pl.BlockSpec(memory_space=pl.ANY)] * unused
    single = not isinstance(out_shape, list)
    outs = pl.BlockSpec(memory_space=out_space)
    return pl.pallas_call(
        kernel,
        out_shape=out_shape,
        in_specs=specs,
        out_specs=outs if single else [outs] * len(out_shape),
        scratch_shapes=list(scratch),
        compiler_params=pltpu.CompilerParams(vmem_limit_bytes=VMEM_LIMIT),
        cost_estimate=pl.CostEstimate(flops=int(gflop * 1e9), bytes_accessed=1 << 20, transcendentals=0),
        name=name,
    )(*operands)


def in_hbm(array):
    return pltpu.with_memory_space_constraint(array, pltpu.HBM)


def across(block, distances):
    heads = lax.axis_size("head")
    devices = [(tile, head) for tile in range(lax.axis_size("tile")) for head in range(heads)]
    route = [(tile * heads + head, (tile ^ distances[head % 2]) * heads + head) for tile, head in devices]
    return lax.ppermute(block, ("tile", "head"), route)


def exchanged(blocks, stride):
    terms = list(blocks[:1])
    for distance in range(1, len(blocks)):
        route = [(tile, tile ^ (distance * stride)) for tile in range(lax.axis_size("tile"))]
        terms.append(lax.ppermute(blocks[distance], "tile", route))
    return terms


def with_partners(blocks, slots):
    tile_count = lax.axis_size("tile")
    routes = {s: [(tile, partner(tile, tile_count, s)) for tile in range(tile_count)] for s in slots}
    return {s: lax.ppermute(blocks[s], "tile", routes[s]) for s in slots}


def shards(queries, keys, values, grad_output, out_weight, rotations):
    tile_count = lax.axis_size("tile")
    token_count, features = queries.shape
    model = out_weight.shape[0]
    pairs = features // PAIR
    far = tile_count // NEAR
    chunk = model // tile_count
    heads = lax.axis_size("head")
    columns = tile_count // 4
    queries, keys, values, out_weight, rotations = (
        in_hbm(a) for a in (queries, keys, values, out_weight, rotations)
    )

    def bf16(*shape):
        return jax.ShapeDtypeStruct(shape, jnp.bfloat16)

    def f32(*shape):
        return jax.ShapeDtypeStruct(shape, jnp.float32)

    strip_types = [bf16(2, STRIP, features)] * 4
    picked = call(
        functools.partial(pick_kernel, columns), "pick_strips", strip_types, (rotations, keys, values), smem=1
    )
    grad_output, *picked = lax.optimization_barrier((grad_output, *picked))
    strips = with_partners(picked, (3, 2, 1, 0))
    strips = [strips[s] for s in range(4)]

    cotangents = [
        lax.ppermute(grad_output, "head", [((h + k) % heads, h) for h in range(heads)]) for k in range(1, heads)
    ]
    dout, dout_turned, turned, turned_sent = call(
        functools.partial(cotangent_kernel, heads),
        "cotangent",
        [bf16(CELLS, features), bf16(features, CELLS)] + [bf16(2, far, chunk, CELLS)] * 2,
        (in_hbm(grad_output), *cotangents, out_weight),
        gflop=1.0,
    )
    turned_arrived = across(turned_sent, (1, 2))
    part_types = [f32(pairs, 2, 2 * CELLS), f32(pairs, HEAD_DIM, 2 * CELLS)]
    raw_centre, stats_centre, sums_centre, product_centre, queries, keys = call(
        centre_kernel,
        "centre",
        [f32(pairs, CELLS, 2 * CELLS)] + part_types + [f32(pairs, CELLS, 2 * CELLS)] + [bf16(CELLS, features)] * 2,
        (queries, keys, values, dout),
        scratch=[pltpu.VMEM((CELLS, CELLS), jnp.float32)],
        gflop=3.0,
    )
    strip_scratch = [pltpu.VMEM((STRIP, CELLS), jnp.float32)]
    raw_columns, stats_columns, sums_columns, product_columns, row_bias, rim_chosen, chosen = call(
        functools.partial(column_kernel, columns),
        "columns",
        [f32(pairs, STRIP, 2 * CELLS)]
        + part_types
        + [f32(pairs, STRIP, 2 * CELLS), f32(STRIP, CELLS), bf16(4, LANES, CELLS), bf16(CELLS, 4 * LANES)],
        (rotations, strips[2], strips[3], queries, dout),
        scratch=strip_scratch,
        smem=1,
        gflop=2.0,
    )
    raw_rows, attention, rows, factors = call(
        row_kernel,
        "rows",
        [f32(pairs, STRIP, 2 * CELLS), bf16(CELLS, features)] + [f32(k, 2 * pairs, CELLS) for k in (3, 2)],
        (strips[0], strips[1], queries, dout_turned, stats_centre, sums_centre, stats_columns, sums_columns, row_bias),
    )
    attention_arrived = across(attention, (1, 2))
    rims = call(
        rim_kernel,
        "rims",
        [bf16(2 * STRIP + 16, features)] * 4,
        (queries, dout, rows, rim_chosen, turned_arrived),
        unused=1,
    )
    rims_arrived = with_partners(rims, (3, 2))
    kept, sent = call(
        partial_kernel,
        "partial",
        [f32(far, chunk, features), bf16(far, chunk, features)],
        (attention, attention_arrived, turned, turned_arrived, rims[0]),
        unused=1,
    )
    terms = [kept, across(sent, (2, 1))]
    rims = lax.optimization_barrier((*rims, sent))[:4]
    rims_arrived |= with_partners(rims, (1, 0))
    grad_queries, centre = call(
        backward_kernel,
        "backward",
        [bf16(CELLS, features), f32(2, CELLS, features)],
        (
            *strips[::-1], queries, keys, dout, raw_centre, raw_columns, raw_rows, product_centre, product_columns,
            rows, factors, sent,
        ),
        unused=1,
        gflop=3.0,
    )
    stride = NEAR
    while stride < tile_count:
        ways = min(NEAR, tile_count // stride)
        sums = call(
            functools.partial(sum_kernel, len(terms)),
            "plane_sum",
            [bf16(tile_count // stride // ways, chunk, features)] * ways,
            (*terms, centre, rims_arrived[3], rims_arrived[2]),
            unused=3,
        )
        terms = exchanged(sums, stride)
        stride *= ways

    grad_keys, grad_values = call(
        side_kernel,
        "sides",
        [bf16(CELLS, features)] * 2,
        (centre, chosen, *(picked[s] for s in SIDE_ORDER), *(rims_arrived[s] for s in SIDE_ORDER)),
        scratch=[pltpu.VMEM((STRIP, LANES), jnp.float32)]
        + [pltpu.VMEM((CELLS, features), jnp.bfloat16)] * 2
        + [pltpu.SemaphoreType.DMA((2 * pairs,))],
        gflop=3.0,
        out_space=pl.ANY,
    )
    grad_out_weight = call(
        functools.partial(weight_kernel, 1.0 / math.sqrt(token_count * tile_count)),
        "weight_sum",
        f32(chunk, features),
        terms,
    )
    return (grad_queries, grad_keys, grad_values, grad_out_weight)


def solution(mesh):
    placed = (
        P("tile", "head"),
        P("tile", "head"),
        P("tile", "head"),
        P("tile", "head"),
        P(None, "head"),
        P("tile", None),
    )
    return jax.shard_map(
        shards,
        mesh=mesh,
        in_specs=placed,
        out_specs=(P("tile", "head"), P("tile", "head"), P("tile", "head"), P("tile", "head")),
        check_vma=False,
    )
```

profile of v0, /device:TPU:0, one launch (start us, length us, event | category | flops | bytes accessed | tf_op | source)
XLA Modules:
  0.0 51.3 jit_solution(1839092320526460150)
XLA Ops:
  0.6 1.5 %pick_strips.1 = (bf16[2,96,512]{2,1,0:T(8,128)(2,1)S(1)}, bf16[2,96,512]{2,1,0:T(8,128)(2,1)S(1)}, bf16[2,96,512]{2,1,0:T(8,128)(2,1)S(1)}, bf16[2,96,512]{2,1,0:T(8,128)(2,1)S(1)}) custom-call(s32[1,4]{1,0:T(1,128)} %rotations_ref.3, bf16[256,512]{1,0:T(8,128)(2,1)} %key_ref.1, bf16[256,512]{1,0:T(8,128)(2,1)} %value_ref.1), custom_call_target="tpu_custom_call" | custom-call | flops 100000000 | bytes 1048576 | tf_op jit(solution)/shard_map/pick_strips/pallas_call | solution.py:505
  2.1 0.5 %collective-permute-start.4 = (bf16[256,512]{1,0:T(8,128)(2,1)}, bf16[256,512]{1,0:T(8,128)(2,1)S(1)}, u32[]{:S(2)}, u32[]{:S(2)}) collective-permute-start(bf16[256,512]{1,0:T(8,128)(2,1)} %refs_0_), channel_id=1, source_target_pairs={{1,0},{0,1},{3,2},{2,3},{5,4},{4,5},{7,6},{6,7},{9,8},{8,9},{11,10... | collective-permute-start | bytes 786440 | tf_op jit(solution)/shard_map/ppermute | solution.py:570
  2.7 4.7 %collective-permute-start = (bf16[2,96,512]{2,1,0:T(8,128)(2,1)S(1)}, bf16[2,96,512]{2,1,0:T(8,128)(2,1)S(1)}, u32[]{:S(2)}, u32[]{:S(2)}) collective-permute-start(bf16[2,96,512]{2,1,0:T(8,128)(2,1)S(1)} %get-tuple-element.54.refs_0_), channel_id=1, source_target_pairs={{0,24},{2,26},{4,28},{6,30},{8,16},{10,18},{12,20},{14,22},{16,8},... | collective-permute-start | bytes 589832 | tf_op jit(solution)/shard_map/ppermute | solution.py:539
  7.3 2.8 %collective-permute-start.2 = (bf16[2,96,512]{2,1,0:T(8,128)(2,1)S(1)}, bf16[2,96,512]{2,1,0:T(8,128)(2,1)S(1)}, u32[]{:S(2)}, u32[]{:S(2)}) collective-permute-start(bf16[2,96,512]{2,1,0:T(8,128)(2,1)S(1)} %get-tuple-element.56.refs_2_), channel_id=1, source_target_pairs={{0,30},{2,4},{4,2},{6,8},{8,6},{10,12},{12,10},{14,16},{16,14},{18... | collective-permute-start | bytes 589832 | tf_op jit(solution)/shard_map/ppermute | solution.py:539
  10.3 2.2 %cotangent.1 = (bf16[256,512]{1,0:T(8,128)(2,1)S(1)}, bf16[512,256]{1,0:T(8,128)(2,1)S(1)}, bf16[2,4,64,256]{3,2,1,0:T(8,128)(2,1)S(1)}, bf16[2,4,64,256]{3,2,1,0:T(8,128)(2,1)S(1)}) custom-call(bf16[256,512]{1,0:T(8,128)(2,1)} %refs_0_, bf16[256,512]{1,0:T(8,128)(2,1)S(1)} %collective-permute-done.4.refs_1_, bf16[1024,512]{1,0:T(8,128)(2,1)} %refs_2_.1), custom_call_target="tpu_custom_call" | custom-call | flops 1000000000 | bytes 1048576 | tf_op jit(solution)/shard_map/cotangent/pallas_call | solution.py:505
  12.5 1.9 %collective-permute-start.6 = (bf16[2,4,64,256]{3,2,1,0:T(8,128)(2,1)S(1)}, bf16[2,4,64,256]{3,2,1,0:T(8,128)(2,1)S(1)}, u32[]{:S(2)}, u32[]{:S(2)}) collective-permute-start(bf16[2,4,64,256]{3,2,1,0:T(8,128)(2,1)S(1)} %get-tuple-element.77), channel_id=1, source_target_pairs={{0,2},{1,5},{2,0},{3,7},{4,6},{5,1},{6,4},{7,3},{8,10},{9,13},{10,... | collective-permute-start | bytes 786440 | tf_op jit(solution)/shard_map/ppermute | solution.py:525
  14.4 3.5 %centre.1 = (f32[4,256,512]{2,1,0:T(8,128)S(1)}, f32[4,2,512]{2,1,0:T(2,128)S(1)}, f32[4,64,512]{2,1,0:T(8,128)S(1)}, f32[4,256,512]{2,1,0:T(8,128)S(1)}, bf16[2...) custom-call(bf16[256,512]{1,0:T(8,128)(2,1)} %query_ref.1, bf16[256,512]{1,0:T(8,128)(2,1)} %key_ref.1, ...), custom_call_target="tpu_custom_call" | custom-call | flops 3000000000 | bytes 1048576 | tf_op jit(solution)/shard_map/centre/pallas_call | solution.py:505
  17.9 3.8 %columns.1 = (f32[4,96,512]{2,1,0:T(8,128)S(1)}, f32[4,2,512]{2,1,0:T(2,128)S(1)}, f32[4,64,512]{2,1,0:T(8,128)S(1)}, f32[4,96,512]{2,1,0:T(8,128)S(1)}, f32[96,...) custom-call(s32[1,4]{1,0:T(1,128)} %rotations_ref.3, ...), custom_call_target="tpu_custom_call" | custom-call | flops 2000000000 | bytes 1048576 | tf_op jit(solution)/shard_map/columns/pallas_call | solution.py:505
  21.7 1.6 %collective-permute-done.2.second_ref = bf16[2,96,512]{2,1,0:T(8,128)(2,1)S(1)} collective-permute-done((bf16[2,96,512]{2,1,0:T(8,128)(2,1)S(1)}, bf16[2,96,512]{2,1,0:T(8,128)(2,1)S(1)}, u32[]{:S(2)}, u32[]{:S(2)}) %collective-permute-start.2) | collective-permute-done | bytes 196640 | tf_op jit(solution)/shard_map/ppermute | solution.py:539
  23.3 2.1 %rows.1 = (f32[4,96,512]{2,1,0:T(8,128)S(1)}, bf16[256,512]{1,0:T(8,128)(2,1)S(1)}, f32[3,8,256]{2,1,0:T(8,128)S(1)}, f32[2,8,256]{2,1,0:T(8,128)S(1)}) custom-call(bf16[2,96,512]{2,1,0:T(8,128)(2,1)S(1)} %collective-permute-done.3.first_ref, bf16[2,96,512]{2,1,0:T(8,128)(2,1)S(1)} %collective-permute-done.2.second_ref, ...), custom_call_target="tpu_custom_call" | custom-call | flops 100000000 | bytes 1048576 | tf_op jit(solution)/shard_map/rows/pallas_call | solution.py:505
  25.5 0.6 %rims.1 = (bf16[208,512]{1,0:T(8,128)(2,1)S(1)}, bf16[208,512]{1,0:T(8,128)(2,1)S(1)}, bf16[208,512]{1,0:T(8,128)(2,1)S(1)}, bf16[208,512]{1,0:T(8,128)(2,1)S(1)}) custom-call(bf16[256,512]{1,0:T(8,128)(2,1)S(1)} %get-tuple-element.60.query_ref, bf16[256,512]{1,0:T(8,128)(2,1)S(1)} %get-tuple-element.59.dout_ref, ...), custom_call_target="tpu_custom_call" | custom-call | flops 100000000 | bytes 1048576 | tf_op jit(solution)/shard_map/rims/pallas_call | solution.py:505
  26.0 1.8 %collective-permute-start.7 = (bf16[208,512]{1,0:T(8,128)(2,1)S(1)}, bf16[208,512]{1,0:T(8,128)(2,1)S(1)}, u32[]{:S(2)}, u32[]{:S(2)}) collective-permute-start(bf16[208,512]{1,0:T(8,128)(2,1)S(1)} %get-tuple-element.84), channel_id=1, source_target_pairs={{0,24},{2,26},{4,28},{6,30},{8,16},{10,18},{12,20},{14,22},{16,8},... | collective-permute-start | bytes 638984 | tf_op jit(solution)/shard_map/ppermute | solution.py:539
  27.9 3.9 %collective-permute-done.5.arrived_ref = bf16[256,512]{1,0:T(8,128)(2,1)S(1)} collective-permute-done((bf16[256,512]{1,0:T(8,128)(2,1)S(1)}, bf16[256,512]{1,0:T(8,128)(2,1)S(1)}, u32[]{:S(2)}, u32[]{:S(2)}) %collective-permute-start.5) | collective-permute-done | bytes 262176 | tf_op jit(solution)/shard_map/ppermute | solution.py:525
  31.8 0.4 partial.1
  32.3 3.5 %collective-permute-start.9 = (bf16[208,512]{1,0:T(8,128)(2,1)S(1)}, bf16[208,512]{1,0:T(8,128)(2,1)S(1)}, u32[]{:S(2)}, u32[]{:S(2)}) collective-permute-start(bf16[208,512]{1,0:T(8,128)(2,1)S(1)} %get-tuple-element.87), channel_id=1, source_target_pairs={{0,30},{2,4},{4,2},{6,8},{8,6},{10,12},{12,10},{14,16},{16,14},{18... | collective-permute-start | bytes 638984 | tf_op jit(solution)/shard_map/ppermute | solution.py:539
  35.8 3.1 %backward.1 = (bf16[256,512]{1,0:T(8,128)(2,1)}, f32[2,256,512]{2,1,0:T(8,128)S(1)}) custom-call(bf16[2,96,512]{2,1,0:T(8,128)(2,1)S(1)} %collective-permute-done.second_ref.fourth_ref, bf16[2,96,512]{2,1,0:T(8,128)(2,1)S(1)} %collective-permute-done.1.first_ref.third_ref, bf16[2,96,512]{2,1,0:T(8,128)(2,1)S(1)} %collective-permute-done.2.second_ref, ...), custom_call_target="tpu_custom_call" | custom-call | flops 3000000000 | bytes 1048576 | tf_op jit(solution)/shard_map/backward/pallas_call | solution.py:505
  39.0 0.5 collective-permute-done.8.refs_5_.refs_4_
  39.4 1.0 %collective-permute-done.11.refs_1_ = bf16[4,64,512]{2,1,0:T(8,128)(2,1)S(1)} collective-permute-done((bf16[4,64,512]{2,1,0:T(8,128)(2,1)S(1)}, bf16[4,64,512]{2,1,0:T(8,128)(2,1)S(1)}, u32[]{:S(2)}, u32[]{:S(2)}) %collective-permute-start.11) | collective-permute-done | bytes 262176 | tf_op jit(solution)/shard_map/ppermute | solution.py:525
  40.5 1.8 %collective-permute-start.12 = (bf16[1,64,512]{2,1,0:T(8,128)(2,1)S(1)}, bf16[1,64,512]{2,1,0:T(8,128)(2,1)S(1)}, u32[]{:S(2)}, u32[]{:S(2)}) collective-permute-start(bf16[1,64,512]{2,1,0:T(8,128)(2,1)S(1)} %get-tuple-element.93), channel_id=1, source_target_pairs={{0,8},{2,10},{4,12},{6,14},{8,0},{10,2},{12,4},{14,6},{16,24},{18,... | collective-permute-start | bytes 196616 | tf_op jit(solution)/shard_map/ppermute | solution.py:532
  42.3 2.1 %collective-permute-start.13 = (bf16[1,64,512]{2,1,0:T(8,128)(2,1)S(1)}, bf16[1,64,512]{2,1,0:T(8,128)(2,1)S(1)}, u32[]{:S(2)}, u32[]{:S(2)}) collective-permute-start(bf16[1,64,512]{2,1,0:T(8,128)(2,1)S(1)} %get-tuple-element.94), channel_id=1, source_target_pairs={{0,16},{2,18},{4,20},{6,22},{8,24},{10,26},{12,28},{14,30},{16,0},... | collective-permute-start | bytes 196616 | tf_op jit(solution)/shard_map/ppermute | solution.py:532
  44.4 1.4 %collective-permute-start.14 = (bf16[1,64,512]{2,1,0:T(8,128)(2,1)S(1)}, bf16[1,64,512]{2,1,0:T(8,128)(2,1)S(1)}, u32[]{:S(2)}, u32[]{:S(2)}) collective-permute-start(bf16[1,64,512]{2,1,0:T(8,128)(2,1)S(1)} %get-tuple-element.95), channel_id=1, source_target_pairs={{0,24},{2,26},{4,28},{6,30},{8,16},{10,18},{12,20},{14,22},{16,8},... | collective-permute-start | bytes 196616 | tf_op jit(solution)/shard_map/ppermute | solution.py:532
  45.8 4.5 %sides.1 = (bf16[256,512]{1,0:T(8,128)(2,1)}, bf16[256,512]{1,0:T(8,128)(2,1)}) custom-call(f32[2,256,512]{2,1,0:T(8,128)S(1)} %get-tuple-element.82.centre_ref.refs_2_, bf16[256,512]{1,0:T(8,128)(2,1)S(1)} %get-tuple-element.83.chosen_ref, bf16[2,96,512]{2,1,0:T(8,128)(2,1)S(1)} %get-tuple-element.54.refs_0_, ...), custom_call_target="tpu_custom_call" | custom-call | flops 3000000000 | bytes 1048576 | tf_op jit(solution)/shard_map/sides/pallas_call | solution.py:505
  50.4 0.2 collective-permute-done.14.refs_3_
  50.6 0.7 %weight_sum.1 = f32[64,512]{1,0:T(8,128)} custom-call(bf16[1,64,512]{2,1,0:T(8,128)(2,1)S(1)} %get-tuple-element.92.refs_0_, bf16[1,64,512]{2,1,0:T(8,128)(2,1)S(1)} %collective-permute-done.12.refs_1_, bf16[1,64,512]{2,1,0:T(8,128)(2,1)S(1)} %collective-permute-done.13.refs_2_, bf16[1,64,512]{2,1,0:T(8,128)(2,1)S(1)} %collective-permute-done.14.refs_3_), custom_call_target="tpu_custom_call" | custom-call | flops 100000000 | bytes 1048576 | tf_op jit(solution)/shard_map/weight_sum/pallas_call | solution.py:505
  (17 shorter events, 0.6 us)
Async XLA Ops:
  2.1 8.2 %collective-permute-start.4 = (bf16[256,512]{1,0:T(8,128)(2,1)}, bf16[256,512]{1,0:T(8,128)(2,1)S(1)}, u32[]{:S(2)}, u32[]{:S(2)}) collective-permute-start(bf16[256,512]{1,0:T(8,128)(2,1)} %refs_0_), channel_id=1, source_target_pairs={{1,0},{0,1},{3,2},{2,3},{5,4},{4,5},{7,6},{6,7},{9,8},{8,9},{11,10... | collective-permute-start | bytes 786440 | tf_op jit(solution)/shard_map/ppermute | solution.py:570
  2.7 15.3 %collective-permute-start = (bf16[2,96,512]{2,1,0:T(8,128)(2,1)S(1)}, bf16[2,96,512]{2,1,0:T(8,128)(2,1)S(1)}, u32[]{:S(2)}, u32[]{:S(2)}) collective-permute-start(bf16[2,96,512]{2,1,0:T(8,128)(2,1)S(1)} %get-tuple-element.54.refs_0_), channel_id=1, source_target_pairs={{0,24},{2,26},{4,28},{6,30},{8,16},{10,18},{12,20},{14,22},{16,8},... | collective-permute-start | bytes 589832 | tf_op jit(solution)/shard_map/ppermute | solution.py:539
  7.3 10.6 %collective-permute-start.1 = (bf16[2,96,512]{2,1,0:T(8,128)(2,1)S(1)}, bf16[2,96,512]{2,1,0:T(8,128)(2,1)S(1)}, u32[]{:S(2)}, u32[]{:S(2)}) collective-permute-start(bf16[2,96,512]{2,1,0:T(8,128)(2,1)S(1)} %get-tuple-element.55.refs_1_), channel_id=1, source_target_pairs={{0,8},{2,10},{4,12},{6,14},{8,0},{10,2},{12,4},{14,6},{16,24},{18,... | collective-permute-start | bytes 589832 | tf_op jit(solution)/shard_map/ppermute | solution.py:539
  7.3 16.0 %collective-permute-start.2 = (bf16[2,96,512]{2,1,0:T(8,128)(2,1)S(1)}, bf16[2,96,512]{2,1,0:T(8,128)(2,1)S(1)}, u32[]{:S(2)}, u32[]{:S(2)}) collective-permute-start(bf16[2,96,512]{2,1,0:T(8,128)(2,1)S(1)} %get-tuple-element.56.refs_2_), channel_id=1, source_target_pairs={{0,30},{2,4},{4,2},{6,8},{8,6},{10,12},{12,10},{14,16},{16,14},{18... | collective-permute-start | bytes 589832 | tf_op jit(solution)/shard_map/ppermute | solution.py:539
  10.1 13.2 %collective-permute-start.3 = (bf16[2,96,512]{2,1,0:T(8,128)(2,1)S(1)}, bf16[2,96,512]{2,1,0:T(8,128)(2,1)S(1)}, u32[]{:S(2)}, u32[]{:S(2)}) collective-permute-start(bf16[2,96,512]{2,1,0:T(8,128)(2,1)S(1)} %get-tuple-element.57.refs_3_), channel_id=1, source_target_pairs={{0,2},{2,0},{4,6},{6,4},{8,10},{10,8},{12,14},{14,12},{16,18},{18,... | collective-permute-start | bytes 589832 | tf_op jit(solution)/shard_map/ppermute | solution.py:539
  12.5 12.9 %collective-permute-start.6 = (bf16[2,4,64,256]{3,2,1,0:T(8,128)(2,1)S(1)}, bf16[2,4,64,256]{3,2,1,0:T(8,128)(2,1)S(1)}, u32[]{:S(2)}, u32[]{:S(2)}) collective-permute-start(bf16[2,4,64,256]{3,2,1,0:T(8,128)(2,1)S(1)} %get-tuple-element.77), channel_id=1, source_target_pairs={{0,2},{1,5},{2,0},{3,7},{4,6},{5,1},{6,4},{7,3},{8,10},{9,13},{10,... | collective-permute-start | bytes 786440 | tf_op jit(solution)/shard_map/ppermute | solution.py:525
  25.4 6.4 %collective-permute-start.5 = (bf16[256,512]{1,0:T(8,128)(2,1)S(1)}, bf16[256,512]{1,0:T(8,128)(2,1)S(1)}, u32[]{:S(2)}, u32[]{:S(2)}) collective-permute-start(bf16[256,512]{1,0:T(8,128)(2,1)S(1)} %get-tuple-element.75.attention_ref), channel_id=1, source_target_pairs={{0,2},{1,5},{2,0},{3,7},{4,6},{5,1},{6,4},{7,3},{8,10},{9,13},{10,... | collective-permute-start | bytes 786440 | tf_op jit(solution)/shard_map/ppermute | solution.py:525
  26.0 12.9 %collective-permute-start.7 = (bf16[208,512]{1,0:T(8,128)(2,1)S(1)}, bf16[208,512]{1,0:T(8,128)(2,1)S(1)}, u32[]{:S(2)}, u32[]{:S(2)}) collective-permute-start(bf16[208,512]{1,0:T(8,128)(2,1)S(1)} %get-tuple-element.84), channel_id=1, source_target_pairs={{0,24},{2,26},{4,28},{6,30},{8,16},{10,18},{12,20},{14,22},{16,8},... | collective-permute-start | bytes 638984 | tf_op jit(solution)/shard_map/ppermute | solution.py:539
  27.8 11.6 %collective-permute-start.8 = (bf16[208,512]{1,0:T(8,128)(2,1)S(1)}, bf16[208,512]{1,0:T(8,128)(2,1)S(1)}, u32[]{:S(2)}, u32[]{:S(2)}) collective-permute-start(bf16[208,512]{1,0:T(8,128)(2,1)S(1)} %get-tuple-element.85), channel_id=1, source_target_pairs={{0,8},{2,10},{4,12},{6,14},{8,0},{10,2},{12,4},{14,6},{16,24},{18,... | collective-permute-start | bytes 638984 | tf_op jit(solution)/shard_map/ppermute | solution.py:539
  32.3 8.2 %collective-permute-start.11 = (bf16[4,64,512]{2,1,0:T(8,128)(2,1)S(1)}, bf16[4,64,512]{2,1,0:T(8,128)(2,1)S(1)}, u32[]{:S(2)}, u32[]{:S(2)}) collective-permute-start(bf16[4,64,512]{2,1,0:T(8,128)(2,1)S(1)} %get-tuple-element.80.unused_ref), channel_id=1, source_target_pairs={{0,4},{1,3},{2,6},{3,1},{4,0},{5,7},{6,2},{7,5},{8,12},{9,11},{10,... | collective-permute-start | bytes 786440 | tf_op jit(solution)/shard_map/ppermute | solution.py:525
  32.3 13.5 %collective-permute-start.9 = (bf16[208,512]{1,0:T(8,128)(2,1)S(1)}, bf16[208,512]{1,0:T(8,128)(2,1)S(1)}, u32[]{:S(2)}, u32[]{:S(2)}) collective-permute-start(bf16[208,512]{1,0:T(8,128)(2,1)S(1)} %get-tuple-element.87), channel_id=1, source_target_pairs={{0,30},{2,4},{4,2},{6,8},{8,6},{10,12},{12,10},{14,16},{16,14},{18... | collective-permute-start | bytes 638984 | tf_op jit(solution)/shard_map/ppermute | solution.py:539
  35.8 10.0 %collective-permute-start.10 = (bf16[208,512]{1,0:T(8,128)(2,1)S(1)}, bf16[208,512]{1,0:T(8,128)(2,1)S(1)}, u32[]{:S(2)}, u32[]{:S(2)}) collective-permute-start(bf16[208,512]{1,0:T(8,128)(2,1)S(1)} %get-tuple-element.88.unused_ref), channel_id=1, source_target_pairs={{0,2},{2,0},{4,6},{6,4},{8,10},{10,8},{12,14},{14,12},{16,18},{18,... | collective-permute-start | bytes 638984 | tf_op jit(solution)/shard_map/ppermute | solution.py:539
  40.5 9.9 %collective-permute-start.12 = (bf16[1,64,512]{2,1,0:T(8,128)(2,1)S(1)}, bf16[1,64,512]{2,1,0:T(8,128)(2,1)S(1)}, u32[]{:S(2)}, u32[]{:S(2)}) collective-permute-start(bf16[1,64,512]{2,1,0:T(8,128)(2,1)S(1)} %get-tuple-element.93), channel_id=1, source_target_pairs={{0,8},{2,10},{4,12},{6,14},{8,0},{10,2},{12,4},{14,6},{16,24},{18,... | collective-permute-start | bytes 196616 | tf_op jit(solution)/shard_map/ppermute | solution.py:532
  42.3 8.1 %collective-permute-start.13 = (bf16[1,64,512]{2,1,0:T(8,128)(2,1)S(1)}, bf16[1,64,512]{2,1,0:T(8,128)(2,1)S(1)}, u32[]{:S(2)}, u32[]{:S(2)}) collective-permute-start(bf16[1,64,512]{2,1,0:T(8,128)(2,1)S(1)} %get-tuple-element.94), channel_id=1, source_target_pairs={{0,16},{2,18},{4,20},{6,22},{8,24},{10,26},{12,28},{14,30},{16,0},... | collective-permute-start | bytes 196616 | tf_op jit(solution)/shard_map/ppermute | solution.py:532
  44.4 6.2 %collective-permute-start.14 = (bf16[1,64,512]{2,1,0:T(8,128)(2,1)S(1)}, bf16[1,64,512]{2,1,0:T(8,128)(2,1)S(1)}, u32[]{:S(2)}, u32[]{:S(2)}) collective-permute-start(bf16[1,64,512]{2,1,0:T(8,128)(2,1)S(1)} %get-tuple-element.95), channel_id=1, source_target_pairs={{0,24},{2,26},{4,28},{6,30},{8,16},{10,18},{12,20},{14,22},{16,8},... | collective-permute-start | bytes 196616 | tf_op jit(solution)/shard_map/ppermute | solution.py:532
where the time goes:
time: 51.5 us; the launch traced here: 51.3 us
  Pallas kernels  22.4 us (43%)
  starting transfers between devices  20.9 us (41%)
  waiting for transfers between devices  7.18 us (14%)
  between operations  0.74 us (1%)
    pallas_call x11, Pallas kernels, call(): pl.pallas_call(kernel, out_shape=out_shape, in_specs=specs, out_specs=out...  22.4 us
    ppermute x8, starting transfers between devices, with_partners(): return {s: lax.ppermute(blocks[s], 'tile', routes[s]) for s in slots}  13 us
    ppermute x3, starting transfers between devices, exchanged(): terms.append(lax.ppermute(blocks[distance], 'tile', route))  5.32 us
    ppermute x3, waiting for transfers between devices, across(): return lax.ppermute(block, ('tile', 'head'), route)  4.87 us
    ppermute x8, waiting for transfers between devices, with_partners(): return {s: lax.ppermute(blocks[s], 'tile', routes[s]) for s in slots}  2.08 us
    ppermute x3, starting transfers between devices, across(): return lax.ppermute(block, ('tile', 'head'), route)  2.03 us
  transfers between devices with their start and end apart: 15, of which 5 were waited for; matrix products, arithmetic and copies ran while one was open for 0% of the time, Pallas kernels for 39%

commit v1 on v0

--- a/solution.py
+++ b/solution.py
@@ -527,7 +527,7 @@
 
 def exchanged(blocks, stride):
     terms = list(blocks[:1])
-    for distance in range(1, len(blocks)):
+    for distance in (2, 3, 1) if len(blocks) == 4 else (1,):
         route = [(tile, tile ^ (distance * stride)) for tile in range(lax.axis_size("tile"))]
         terms.append(lax.ppermute(blocks[distance], "tile", route))
     return terms

time: 51.5 us -> 51.3 us (level)
  starting transfers between devices: 20.9 us -> 20.1 us
  waiting for transfers between devices: 7.18 us -> 7.83 us
    ppermute x3, starting transfers between devices: 5.32 us -> 4.49 us  [exchanged(): terms.append(lax.ppermute(blocks[distance], 'tile', route))]
    ppermute x8, waiting for transfers between devices: 2.08 us -> 2.75 us  [with_partners(): return {s: lax.ppermute(blocks[s], 'tile', routes[s]) for s in slots}]
  transfers between devices with their start and end apart: 15 -> 15, of which waited for: 5 -> 6; matrix products, arithmetic and copies ran while one was open for 0% -> 0% of each run, Pallas kernels for 39% -> 40%
where the time goes in v1:
time: 51.3 us; the launch traced here: 51.1 us
  Pallas kernels  22.4 us (44%)
  starting transfers between devices  20.1 us (39%)
  waiting for transfers between devices  7.83 us (15%)
  between operations  0.74 us (1%)
    pallas_call x11, Pallas kernels, call(): pl.pallas_call(kernel, out_shape=out_shape, in_specs=specs, out_specs=out...  22.4 us
    ppermute x8, starting transfers between devices, with_partners(): return {s: lax.ppermute(blocks[s], 'tile', routes[s]) for s in slots}  13 us
    ppermute x3, waiting for transfers between devices, across(): return lax.ppermute(block, ('tile', 'head'), route)  4.87 us
    ppermute x3, starting transfers between devices, exchanged(): terms.append(lax.ppermute(blocks[distance], 'tile', route))  4.49 us
    ppermute x8, waiting for transfers between devices, with_partners(): return {s: lax.ppermute(blocks[s], 'tile', routes[s]) for s in slots}  2.75 us
    ppermute x3, starting transfers between devices, across(): return lax.ppermute(block, ('tile', 'head'), route)  2.03 us
  transfers between devices with their start and end apart: 15, of which 6 were waited for; matrix products, arithmetic and copies ran while one was open for 0% of the time, Pallas kernels for 40%

profile of v1, /device:TPU:0, one launch (start us, length us, event | category | flops | bytes accessed | tf_op | source)
XLA Modules:
  0.0 51.1 jit_solution(12745595069315059373)
XLA Ops:
  0.6 1.5 %pick_strips.1 = (bf16[2,96,512]{2,1,0:T(8,128)(2,1)S(1)}, bf16[2,96,512]{2,1,0:T(8,128)(2,1)S(1)}, bf16[2,96,512]{2,1,0:T(8,128)(2,1)S(1)}, bf16[2,96,512]{2,1,0:T(8,128)(2,1)S(1)}) custom-call(s32[1,4]{1,0:T(1,128)} %rotations_ref.3, bf16[256,512]{1,0:T(8,128)(2,1)} %key_ref.1, bf16[256,512]{1,0:T(8,128)(2,1)} %value_ref.1), custom_call_target="tpu_custom_call" | custom-call | flops 100000000 | bytes 1048576 | tf_op jit(solution)/shard_map/pick_strips/pallas_call | solution.py:505
  2.1 0.5 %collective-permute-start.4 = (bf16[256,512]{1,0:T(8,128)(2,1)}, bf16[256,512]{1,0:T(8,128)(2,1)S(1)}, u32[]{:S(2)}, u32[]{:S(2)}) collective-permute-start(bf16[256,512]{1,0:T(8,128)(2,1)} %refs_0_), channel_id=1, source_target_pairs={{1,0},{0,1},{3,2},{2,3},{5,4},{4,5},{7,6},{6,7},{9,8},{8,9},{11,10... | collective-permute-start | bytes 786440 | tf_op jit(solution)/shard_map/ppermute | solution.py:570
  2.7 4.7 %collective-permute-start = (bf16[2,96,512]{2,1,0:T(8,128)(2,1)S(1)}, bf16[2,96,512]{2,1,0:T(8,128)(2,1)S(1)}, u32[]{:S(2)}, u32[]{:S(2)}) collective-permute-start(bf16[2,96,512]{2,1,0:T(8,128)(2,1)S(1)} %get-tuple-element.54.refs_0_), channel_id=1, source_target_pairs={{0,24},{2,26},{4,28},{6,30},{8,16},{10,18},{12,20},{14,22},{16,8},... | collective-permute-start | bytes 589832 | tf_op jit(solution)/shard_map/ppermute | solution.py:539
  7.3 2.8 %collective-permute-start.2 = (bf16[2,96,512]{2,1,0:T(8,128)(2,1)S(1)}, bf16[2,96,512]{2,1,0:T(8,128)(2,1)S(1)}, u32[]{:S(2)}, u32[]{:S(2)}) collective-permute-start(bf16[2,96,512]{2,1,0:T(8,128)(2,1)S(1)} %get-tuple-element.56.refs_2_), channel_id=1, source_target_pairs={{0,30},{2,4},{4,2},{6,8},{8,6},{10,12},{12,10},{14,16},{16,14},{18... | collective-permute-start | bytes 589832 | tf_op jit(solution)/shard_map/ppermute | solution.py:539
  10.3 2.2 %cotangent.1 = (bf16[256,512]{1,0:T(8,128)(2,1)S(1)}, bf16[512,256]{1,0:T(8,128)(2,1)S(1)}, bf16[2,4,64,256]{3,2,1,0:T(8,128)(2,1)S(1)}, bf16[2,4,64,256]{3,2,1,0:T(8,128)(2,1)S(1)}) custom-call(bf16[256,512]{1,0:T(8,128)(2,1)} %refs_0_, bf16[256,512]{1,0:T(8,128)(2,1)S(1)} %collective-permute-done.4.refs_1_, bf16[1024,512]{1,0:T(8,128)(2,1)} %refs_2_.1), custom_call_target="tpu_custom_call" | custom-call | flops 1000000000 | bytes 1048576 | tf_op jit(solution)/shard_map/cotangent/pallas_call | solution.py:505
  12.5 1.9 %collective-permute-start.6 = (bf16[2,4,64,256]{3,2,1,0:T(8,128)(2,1)S(1)}, bf16[2,4,64,256]{3,2,1,0:T(8,128)(2,1)S(1)}, u32[]{:S(2)}, u32[]{:S(2)}) collective-permute-start(bf16[2,4,64,256]{3,2,1,0:T(8,128)(2,1)S(1)} %get-tuple-element.77), channel_id=1, source_target_pairs={{0,2},{1,5},{2,0},{3,7},{4,6},{5,1},{6,4},{7,3},{8,10},{9,13},{10,... | collective-permute-start | bytes 786440 | tf_op jit(solution)/shard_map/ppermute | solution.py:525
  14.4 3.5 %centre.1 = (f32[4,256,512]{2,1,0:T(8,128)S(1)}, f32[4,2,512]{2,1,0:T(2,128)S(1)}, f32[4,64,512]{2,1,0:T(8,128)S(1)}, f32[4,256,512]{2,1,0:T(8,128)S(1)}, bf16[2...) custom-call(bf16[256,512]{1,0:T(8,128)(2,1)} %query_ref.1, bf16[256,512]{1,0:T(8,128)(2,1)} %key_ref.1, ...), custom_call_target="tpu_custom_call" | custom-call | flops 3000000000 | bytes 1048576 | tf_op jit(solution)/shard_map/centre/pallas_call | solution.py:505
  17.9 3.8 %columns.1 = (f32[4,96,512]{2,1,0:T(8,128)S(1)}, f32[4,2,512]{2,1,0:T(2,128)S(1)}, f32[4,64,512]{2,1,0:T(8,128)S(1)}, f32[4,96,512]{2,1,0:T(8,128)S(1)}, f32[96,...) custom-call(s32[1,4]{1,0:T(1,128)} %rotations_ref.3, ...), custom_call_target="tpu_custom_call" | custom-call | flops 2000000000 | bytes 1048576 | tf_op jit(solution)/shard_map/columns/pallas_call | solution.py:505
  21.7 1.6 %collective-permute-done.2.second_ref = bf16[2,96,512]{2,1,0:T(8,128)(2,1)S(1)} collective-permute-done((bf16[2,96,512]{2,1,0:T(8,128)(2,1)S(1)}, bf16[2,96,512]{2,1,0:T(8,128)(2,1)S(1)}, u32[]{:S(2)}, u32[]{:S(2)}) %collective-permute-start.2) | collective-permute-done | bytes 196640 | tf_op jit(solution)/shard_map/ppermute | solution.py:539
  23.3 2.1 %rows.1 = (f32[4,96,512]{2,1,0:T(8,128)S(1)}, bf16[256,512]{1,0:T(8,128)(2,1)S(1)}, f32[3,8,256]{2,1,0:T(8,128)S(1)}, f32[2,8,256]{2,1,0:T(8,128)S(1)}) custom-call(bf16[2,96,512]{2,1,0:T(8,128)(2,1)S(1)} %collective-permute-done.3.first_ref, bf16[2,96,512]{2,1,0:T(8,128)(2,1)S(1)} %collective-permute-done.2.second_ref, ...), custom_call_target="tpu_custom_call" | custom-call | flops 100000000 | bytes 1048576 | tf_op jit(solution)/shard_map/rows/pallas_call | solution.py:505
  25.5 0.6 %rims.1 = (bf16[208,512]{1,0:T(8,128)(2,1)S(1)}, bf16[208,512]{1,0:T(8,128)(2,1)S(1)}, bf16[208,512]{1,0:T(8,128)(2,1)S(1)}, bf16[208,512]{1,0:T(8,128)(2,1)S(1)}) custom-call(bf16[256,512]{1,0:T(8,128)(2,1)S(1)} %get-tuple-element.60.query_ref, bf16[256,512]{1,0:T(8,128)(2,1)S(1)} %get-tuple-element.59.dout_ref, ...), custom_call_target="tpu_custom_call" | custom-call | flops 100000000 | bytes 1048576 | tf_op jit(solution)/shard_map/rims/pallas_call | solution.py:505
  26.0 1.8 %collective-permute-start.7 = (bf16[208,512]{1,0:T(8,128)(2,1)S(1)}, bf16[208,512]{1,0:T(8,128)(2,1)S(1)}, u32[]{:S(2)}, u32[]{:S(2)}) collective-permute-start(bf16[208,512]{1,0:T(8,128)(2,1)S(1)} %get-tuple-element.84), channel_id=1, source_target_pairs={{0,24},{2,26},{4,28},{6,30},{8,16},{10,18},{12,20},{14,22},{16,8},... | collective-permute-start | bytes 638984 | tf_op jit(solution)/shard_map/ppermute | solution.py:539
  27.9 3.9 %collective-permute-done.5.arrived_ref = bf16[256,512]{1,0:T(8,128)(2,1)S(1)} collective-permute-done((bf16[256,512]{1,0:T(8,128)(2,1)S(1)}, bf16[256,512]{1,0:T(8,128)(2,1)S(1)}, u32[]{:S(2)}, u32[]{:S(2)}) %collective-permute-start.5) | collective-permute-done | bytes 262176 | tf_op jit(solution)/shard_map/ppermute | solution.py:525
  31.8 0.4 partial.1
  32.3 3.5 %collective-permute-start.9 = (bf16[208,512]{1,0:T(8,128)(2,1)S(1)}, bf16[208,512]{1,0:T(8,128)(2,1)S(1)}, u32[]{:S(2)}, u32[]{:S(2)}) collective-permute-start(bf16[208,512]{1,0:T(8,128)(2,1)S(1)} %get-tuple-element.87), channel_id=1, source_target_pairs={{0,30},{2,4},{4,2},{6,8},{8,6},{10,12},{12,10},{14,16},{16,14},{18... | collective-permute-start | bytes 638984 | tf_op jit(solution)/shard_map/ppermute | solution.py:539
  35.8 3.1 %backward.1 = (bf16[256,512]{1,0:T(8,128)(2,1)}, f32[2,256,512]{2,1,0:T(8,128)S(1)}) custom-call(bf16[2,96,512]{2,1,0:T(8,128)(2,1)S(1)} %collective-permute-done.second_ref.fourth_ref, bf16[2,96,512]{2,1,0:T(8,128)(2,1)S(1)} %collective-permute-done.1.first_ref.third_ref, bf16[2,96,512]{2,1,0:T(8,128)(2,1)S(1)} %collective-permute-done.2.second_ref, ...), custom_call_target="tpu_custom_call" | custom-call | flops 3000000000 | bytes 1048576 | tf_op jit(solution)/shard_map/backward/pallas_call | solution.py:505
  39.0 0.5 collective-permute-done.8.refs_5_.refs_4_
  39.4 1.0 %collective-permute-done.11.refs_1_ = bf16[4,64,512]{2,1,0:T(8,128)(2,1)S(1)} collective-permute-done((bf16[4,64,512]{2,1,0:T(8,128)(2,1)S(1)}, bf16[4,64,512]{2,1,0:T(8,128)(2,1)S(1)}, u32[]{:S(2)}, u32[]{:S(2)}) %collective-permute-start.11) | collective-permute-done | bytes 262176 | tf_op jit(solution)/shard_map/ppermute | solution.py:525
  40.5 3.9 %collective-permute-start.12 = (bf16[1,64,512]{2,1,0:T(8,128)(2,1)S(1)}, bf16[1,64,512]{2,1,0:T(8,128)(2,1)S(1)}, u32[]{:S(2)}, u32[]{:S(2)}) collective-permute-start(bf16[1,64,512]{2,1,0:T(8,128)(2,1)S(1)} %get-tuple-element.93), channel_id=1, source_target_pairs={{0,16},{2,18},{4,20},{6,22},{8,24},{10,26},{12,28},{14,30},{16,0},... | collective-permute-start | bytes 196616 | tf_op jit(solution)/shard_map/ppermute | solution.py:532
  44.3 0.3 collective-permute-start.13
  44.7 0.3 collective-permute-start.14
  45.0 0.6 %collective-permute-done.10.refs_7_ = bf16[208,512]{1,0:T(8,128)(2,1)S(1)} collective-permute-done((bf16[208,512]{1,0:T(8,128)(2,1)S(1)}, bf16[208,512]{1,0:T(8,128)(2,1)S(1)}, u32[]{:S(2)}, u32[]{:S(2)}) %collective-permute-start.10) | collective-permute-done | bytes 213024 | tf_op jit(solution)/shard_map/ppermute | solution.py:539
  45.6 4.5 %sides.1 = (bf16[256,512]{1,0:T(8,128)(2,1)}, bf16[256,512]{1,0:T(8,128)(2,1)}) custom-call(f32[2,256,512]{2,1,0:T(8,128)S(1)} %get-tuple-element.82.centre_ref.refs_2_, bf16[256,512]{1,0:T(8,128)(2,1)S(1)} %get-tuple-element.83.chosen_ref, bf16[2,96,512]{2,1,0:T(8,128)(2,1)S(1)} %get-tuple-element.54.refs_0_, ...), custom_call_target="tpu_custom_call" | custom-call | flops 3000000000 | bytes 1048576 | tf_op jit(solution)/shard_map/sides/pallas_call | solution.py:505
  50.4 0.7 %weight_sum.1 = f32[64,512]{1,0:T(8,128)} custom-call(bf16[1,64,512]{2,1,0:T(8,128)(2,1)S(1)} %get-tuple-element.92.refs_0_, bf16[1,64,512]{2,1,0:T(8,128)(2,1)S(1)} %collective-permute-done.12.refs_1_, bf16[1,64,512]{2,1,0:T(8,128)(2,1)S(1)} %collective-permute-done.13.refs_2_, bf16[1,64,512]{2,1,0:T(8,128)(2,1)S(1)} %collective-permute-done.14.refs_3_), custom_call_target="tpu_custom_call" | custom-call | flops 100000000 | bytes 1048576 | tf_op jit(solution)/shard_map/weight_sum/pallas_call | solution.py:505
  (17 shorter events, 0.8 us)
Async XLA Ops:
  2.1 8.2 %collective-permute-start.4 = (bf16[256,512]{1,0:T(8,128)(2,1)}, bf16[256,512]{1,0:T(8,128)(2,1)S(1)}, u32[]{:S(2)}, u32[]{:S(2)}) collective-permute-start(bf16[256,512]{1,0:T(8,128)(2,1)} %refs_0_), channel_id=1, source_target_pairs={{1,0},{0,1},{3,2},{2,3},{5,4},{4,5},{7,6},{6,7},{9,8},{8,9},{11,10... | collective-permute-start | bytes 786440 | tf_op jit(solution)/shard_map/ppermute | solution.py:570
  2.7 15.3 %collective-permute-start = (bf16[2,96,512]{2,1,0:T(8,128)(2,1)S(1)}, bf16[2,96,512]{2,1,0:T(8,128)(2,1)S(1)}, u32[]{:S(2)}, u32[]{:S(2)}) collective-permute-start(bf16[2,96,512]{2,1,0:T(8,128)(2,1)S(1)} %get-tuple-element.54.refs_0_), channel_id=1, source_target_pairs={{0,24},{2,26},{4,28},{6,30},{8,16},{10,18},{12,20},{14,22},{16,8},... | collective-permute-start | bytes 589832 | tf_op jit(solution)/shard_map/ppermute | solution.py:539
  7.3 10.6 %collective-permute-start.1 = (bf16[2,96,512]{2,1,0:T(8,128)(2,1)S(1)}, bf16[2,96,512]{2,1,0:T(8,128)(2,1)S(1)}, u32[]{:S(2)}, u32[]{:S(2)}) collective-permute-start(bf16[2,96,512]{2,1,0:T(8,128)(2,1)S(1)} %get-tuple-element.55.refs_1_), channel_id=1, source_target_pairs={{0,8},{2,10},{4,12},{6,14},{8,0},{10,2},{12,4},{14,6},{16,24},{18,... | collective-permute-start | bytes 589832 | tf_op jit(solution)/shard_map/ppermute | solution.py:539
  7.3 16.0 %collective-permute-start.2 = (bf16[2,96,512]{2,1,0:T(8,128)(2,1)S(1)}, bf16[2,96,512]{2,1,0:T(8,128)(2,1)S(1)}, u32[]{:S(2)}, u32[]{:S(2)}) collective-permute-start(bf16[2,96,512]{2,1,0:T(8,128)(2,1)S(1)} %get-tuple-element.56.refs_2_), channel_id=1, source_target_pairs={{0,30},{2,4},{4,2},{6,8},{8,6},{10,12},{12,10},{14,16},{16,14},{18... | collective-permute-start | bytes 589832 | tf_op jit(solution)/shard_map/ppermute | solution.py:539
  10.1 13.2 %collective-permute-start.3 = (bf16[2,96,512]{2,1,0:T(8,128)(2,1)S(1)}, bf16[2,96,512]{2,1,0:T(8,128)(2,1)S(1)}, u32[]{:S(2)}, u32[]{:S(2)}) collective-permute-start(bf16[2,96,512]{2,1,0:T(8,128)(2,1)S(1)} %get-tuple-element.57.refs_3_), channel_id=1, source_target_pairs={{0,2},{2,0},{4,6},{6,4},{8,10},{10,8},{12,14},{14,12},{16,18},{18,... | collective-permute-start | bytes 589832 | tf_op jit(solution)/shard_map/ppermute | solution.py:539
  12.5 12.9 %collective-permute-start.6 = (bf16[2,4,64,256]{3,2,1,0:T(8,128)(2,1)S(1)}, bf16[2,4,64,256]{3,2,1,0:T(8,128)(2,1)S(1)}, u32[]{:S(2)}, u32[]{:S(2)}) collective-permute-start(bf16[2,4,64,256]{3,2,1,0:T(8,128)(2,1)S(1)} %get-tuple-element.77), channel_id=1, source_target_pairs={{0,2},{1,5},{2,0},{3,7},{4,6},{5,1},{6,4},{7,3},{8,10},{9,13},{10,... | collective-permute-start | bytes 786440 | tf_op jit(solution)/shard_map/ppermute | solution.py:525
  25.4 6.4 %collective-permute-start.5 = (bf16[256,512]{1,0:T(8,128)(2,1)S(1)}, bf16[256,512]{1,0:T(8,128)(2,1)S(1)}, u32[]{:S(2)}, u32[]{:S(2)}) collective-permute-start(bf16[256,512]{1,0:T(8,128)(2,1)S(1)} %get-tuple-element.75.attention_ref), channel_id=1, source_target_pairs={{0,2},{1,5},{2,0},{3,7},{4,6},{5,1},{6,4},{7,3},{8,10},{9,13},{10,... | collective-permute-start | bytes 786440 | tf_op jit(solution)/shard_map/ppermute | solution.py:525
  26.0 12.9 %collective-permute-start.7 = (bf16[208,512]{1,0:T(8,128)(2,1)S(1)}, bf16[208,512]{1,0:T(8,128)(2,1)S(1)}, u32[]{:S(2)}, u32[]{:S(2)}) collective-permute-start(bf16[208,512]{1,0:T(8,128)(2,1)S(1)} %get-tuple-element.84), channel_id=1, source_target_pairs={{0,24},{2,26},{4,28},{6,30},{8,16},{10,18},{12,20},{14,22},{16,8},... | collective-permute-start | bytes 638984 | tf_op jit(solution)/shard_map/ppermute | solution.py:539
  27.8 11.6 %collective-permute-start.8 = (bf16[208,512]{1,0:T(8,128)(2,1)S(1)}, bf16[208,512]{1,0:T(8,128)(2,1)S(1)}, u32[]{:S(2)}, u32[]{:S(2)}) collective-permute-start(bf16[208,512]{1,0:T(8,128)(2,1)S(1)} %get-tuple-element.85), channel_id=1, source_target_pairs={{0,8},{2,10},{4,12},{6,14},{8,0},{10,2},{12,4},{14,6},{16,24},{18,... | collective-permute-start | bytes 638984 | tf_op jit(solution)/shard_map/ppermute | solution.py:539
  32.3 8.2 %collective-permute-start.11 = (bf16[4,64,512]{2,1,0:T(8,128)(2,1)S(1)}, bf16[4,64,512]{2,1,0:T(8,128)(2,1)S(1)}, u32[]{:S(2)}, u32[]{:S(2)}) collective-permute-start(bf16[4,64,512]{2,1,0:T(8,128)(2,1)S(1)} %get-tuple-element.80.unused_ref), channel_id=1, source_target_pairs={{0,4},{1,3},{2,6},{3,1},{4,0},{5,7},{6,2},{7,5},{8,12},{9,11},{10,... | collective-permute-start | bytes 786440 | tf_op jit(solution)/shard_map/ppermute | solution.py:525
  32.3 12.7 %collective-permute-start.9 = (bf16[208,512]{1,0:T(8,128)(2,1)S(1)}, bf16[208,512]{1,0:T(8,128)(2,1)S(1)}, u32[]{:S(2)}, u32[]{:S(2)}) collective-permute-start(bf16[208,512]{1,0:T(8,128)(2,1)S(1)} %get-tuple-element.87), channel_id=1, source_target_pairs={{0,30},{2,4},{4,2},{6,8},{8,6},{10,12},{12,10},{14,16},{16,14},{18... | collective-permute-start | bytes 638984 | tf_op jit(solution)/shard_map/ppermute | solution.py:539
  35.8 9.8 %collective-permute-start.10 = (bf16[208,512]{1,0:T(8,128)(2,1)S(1)}, bf16[208,512]{1,0:T(8,128)(2,1)S(1)}, u32[]{:S(2)}, u32[]{:S(2)}) collective-permute-start(bf16[208,512]{1,0:T(8,128)(2,1)S(1)} %get-tuple-element.88.unused_ref), channel_id=1, source_target_pairs={{0,2},{2,0},{4,6},{6,4},{8,10},{10,8},{12,14},{14,12},{16,18},{18,... | collective-permute-start | bytes 638984 | tf_op jit(solution)/shard_map/ppermute | solution.py:539
  40.5 9.7 %collective-permute-start.12 = (bf16[1,64,512]{2,1,0:T(8,128)(2,1)S(1)}, bf16[1,64,512]{2,1,0:T(8,128)(2,1)S(1)}, u32[]{:S(2)}, u32[]{:S(2)}) collective-permute-start(bf16[1,64,512]{2,1,0:T(8,128)(2,1)S(1)} %get-tuple-element.93), channel_id=1, source_target_pairs={{0,16},{2,18},{4,20},{6,22},{8,24},{10,26},{12,28},{14,30},{16,0},... | collective-permute-start | bytes 196616 | tf_op jit(solution)/shard_map/ppermute | solution.py:532
  44.3 6.1 %collective-permute-start.13 = (bf16[1,64,512]{2,1,0:T(8,128)(2,1)S(1)}, bf16[1,64,512]{2,1,0:T(8,128)(2,1)S(1)}, u32[]{:S(2)}, u32[]{:S(2)}) collective-permute-start(bf16[1,64,512]{2,1,0:T(8,128)(2,1)S(1)} %get-tuple-element.94), channel_id=1, source_target_pairs={{0,24},{2,26},{4,28},{6,30},{8,16},{10,18},{12,20},{14,22},{16,8},... | collective-permute-start | bytes 196616 | tf_op jit(solution)/shard_map/ppermute | solution.py:532
  44.7 5.7 %collective-permute-start.14 = (bf16[1,64,512]{2,1,0:T(8,128)(2,1)S(1)}, bf16[1,64,512]{2,1,0:T(8,128)(2,1)S(1)}, u32[]{:S(2)}, u32[]{:S(2)}) collective-permute-start(bf16[1,64,512]{2,1,0:T(8,128)(2,1)S(1)} %get-tuple-element.95), channel_id=1, source_target_pairs={{0,8},{2,10},{4,12},{6,14},{8,0},{10,2},{12,4},{14,6},{16,24},{18,... | collective-permute-start | bytes 196616 | tf_op jit(solution)/shard_map/ppermute | solution.py:532

commit v2 on v1

--- a/solution.py
+++ b/solution.py
@@ -527,7 +527,7 @@
 
 def exchanged(blocks, stride):
     terms = list(blocks[:1])
-    for distance in (2, 3, 1) if len(blocks) == 4 else (1,):
+    for distance in (3, 2, 1) if len(blocks) == 4 else (1,):
         route = [(tile, tile ^ (distance * stride)) for tile in range(lax.axis_size("tile"))]
         terms.append(lax.ppermute(blocks[distance], "tile", route))
     return terms

time: 51.3 us -> 51.1 us (level)
  transfers between devices with their start and end apart: 15 -> 15, of which waited for: 6 -> 5; matrix products, arithmetic and copies ran while one was open for 0% -> 0% of each run, Pallas kernels for 40% -> 40%
where the time goes in v2:
time: 51.1 us; the launch traced here: 50.9 us
  Pallas kernels  22.4 us (44%)
  starting transfers between devices  20 us (39%)
  waiting for transfers between devices  7.67 us (15%)
  between operations  0.75 us (1%)
    pallas_call x11, Pallas kernels, call(): pl.pallas_call(kernel, out_shape=out_shape, in_specs=specs, out_specs=out...  22.4 us
    ppermute x8, starting transfers between devices, with_partners(): return {s: lax.ppermute(blocks[s], 'tile', routes[s]) for s in slots}  13 us
    ppermute x3, waiting for transfers between devices, across(): return lax.ppermute(block, ('tile', 'head'), route)  4.87 us
    ppermute x3, starting transfers between devices, exchanged(): terms.append(lax.ppermute(blocks[distance], 'tile', route))  4.45 us
    ppermute x8, waiting for transfers between devices, with_partners(): return {s: lax.ppermute(blocks[s], 'tile', routes[s]) for s in slots}  2.79 us
    ppermute x3, starting transfers between devices, across(): return lax.ppermute(block, ('tile', 'head'), route)  2.03 us
  transfers between devices with their start and end apart: 15, of which 5 were waited for; matrix products, arithmetic and copies ran while one was open for 0% of the time, Pallas kernels for 40%

profile of v2, /device:TPU:0, one launch (start us, length us, event | category | flops | bytes accessed | tf_op | source)
XLA Modules:
  0.0 50.9 jit_solution(695730614562885716)
XLA Ops:
  0.6 1.5 %pick_strips.1 = (bf16[2,96,512]{2,1,0:T(8,128)(2,1)S(1)}, bf16[2,96,512]{2,1,0:T(8,128)(2,1)S(1)}, bf16[2,96,512]{2,1,0:T(8,128)(2,1)S(1)}, bf16[2,96,512]{2,1,0:T(8,128)(2,1)S(1)}) custom-call(s32[1,4]{1,0:T(1,128)} %rotations_ref.3, bf16[256,512]{1,0:T(8,128)(2,1)} %key_ref.1, bf16[256,512]{1,0:T(8,128)(2,1)} %value_ref.1), custom_call_target="tpu_custom_call" | custom-call | flops 100000000 | bytes 1048576 | tf_op jit(solution)/shard_map/pick_strips/pallas_call | solution.py:505
  2.1 0.5 %collective-permute-start.4 = (bf16[256,512]{1,0:T(8,128)(2,1)}, bf16[256,512]{1,0:T(8,128)(2,1)S(1)}, u32[]{:S(2)}, u32[]{:S(2)}) collective-permute-start(bf16[256,512]{1,0:T(8,128)(2,1)} %refs_0_), channel_id=1, source_target_pairs={{1,0},{0,1},{3,2},{2,3},{5,4},{4,5},{7,6},{6,7},{9,8},{8,9},{11,10... | collective-permute-start | bytes 786440 | tf_op jit(solution)/shard_map/ppermute | solution.py:570
  2.7 4.7 %collective-permute-start = (bf16[2,96,512]{2,1,0:T(8,128)(2,1)S(1)}, bf16[2,96,512]{2,1,0:T(8,128)(2,1)S(1)}, u32[]{:S(2)}, u32[]{:S(2)}) collective-permute-start(bf16[2,96,512]{2,1,0:T(8,128)(2,1)S(1)} %get-tuple-element.54.refs_0_), channel_id=1, source_target_pairs={{0,24},{2,26},{4,28},{6,30},{8,16},{10,18},{12,20},{14,22},{16,8},... | collective-permute-start | bytes 589832 | tf_op jit(solution)/shard_map/ppermute | solution.py:539
  7.3 2.8 %collective-permute-start.2 = (bf16[2,96,512]{2,1,0:T(8,128)(2,1)S(1)}, bf16[2,96,512]{2,1,0:T(8,128)(2,1)S(1)}, u32[]{:S(2)}, u32[]{:S(2)}) collective-permute-start(bf16[2,96,512]{2,1,0:T(8,128)(2,1)S(1)} %get-tuple-element.56.refs_2_), channel_id=1, source_target_pairs={{0,30},{2,4},{4,2},{6,8},{8,6},{10,12},{12,10},{14,16},{16,14},{18... | collective-permute-start | bytes 589832 | tf_op jit(solution)/shard_map/ppermute | solution.py:539
  10.3 2.2 %cotangent.1 = (bf16[256,512]{1,0:T(8,128)(2,1)S(1)}, bf16[512,256]{1,0:T(8,128)(2,1)S(1)}, bf16[2,4,64,256]{3,2,1,0:T(8,128)(2,1)S(1)}, bf16[2,4,64,256]{3,2,1,0:T(8,128)(2,1)S(1)}) custom-call(bf16[256,512]{1,0:T(8,128)(2,1)} %refs_0_, bf16[256,512]{1,0:T(8,128)(2,1)S(1)} %collective-permute-done.4.refs_1_, bf16[1024,512]{1,0:T(8,128)(2,1)} %refs_2_.1), custom_call_target="tpu_custom_call" | custom-call | flops 1000000000 | bytes 1048576 | tf_op jit(solution)/shard_map/cotangent/pallas_call | solution.py:505
  12.5 1.9 %collective-permute-start.6 = (bf16[2,4,64,256]{3,2,1,0:T(8,128)(2,1)S(1)}, bf16[2,4,64,256]{3,2,1,0:T(8,128)(2,1)S(1)}, u32[]{:S(2)}, u32[]{:S(2)}) collective-permute-start(bf16[2,4,64,256]{3,2,1,0:T(8,128)(2,1)S(1)} %get-tuple-element.77), channel_id=1, source_target_pairs={{0,2},{1,5},{2,0},{3,7},{4,6},{5,1},{6,4},{7,3},{8,10},{9,13},{10,... | collective-permute-start | bytes 786440 | tf_op jit(solution)/shard_map/ppermute | solution.py:525
  14.4 3.5 %centre.1 = (f32[4,256,512]{2,1,0:T(8,128)S(1)}, f32[4,2,512]{2,1,0:T(2,128)S(1)}, f32[4,64,512]{2,1,0:T(8,128)S(1)}, f32[4,256,512]{2,1,0:T(8,128)S(1)}, bf16[2...) custom-call(bf16[256,512]{1,0:T(8,128)(2,1)} %query_ref.1, bf16[256,512]{1,0:T(8,128)(2,1)} %key_ref.1, ...), custom_call_target="tpu_custom_call" | custom-call | flops 3000000000 | bytes 1048576 | tf_op jit(solution)/shard_map/centre/pallas_call | solution.py:505
  17.9 3.8 %columns.1 = (f32[4,96,512]{2,1,0:T(8,128)S(1)}, f32[4,2,512]{2,1,0:T(2,128)S(1)}, f32[4,64,512]{2,1,0:T(8,128)S(1)}, f32[4,96,512]{2,1,0:T(8,128)S(1)}, f32[96,...) custom-call(s32[1,4]{1,0:T(1,128)} %rotations_ref.3, ...), custom_call_target="tpu_custom_call" | custom-call | flops 2000000000 | bytes 1048576 | tf_op jit(solution)/shard_map/columns/pallas_call | solution.py:505
  21.7 1.6 %collective-permute-done.2.second_ref = bf16[2,96,512]{2,1,0:T(8,128)(2,1)S(1)} collective-permute-done((bf16[2,96,512]{2,1,0:T(8,128)(2,1)S(1)}, bf16[2,96,512]{2,1,0:T(8,128)(2,1)S(1)}, u32[]{:S(2)}, u32[]{:S(2)}) %collective-permute-start.2) | collective-permute-done | bytes 196640 | tf_op jit(solution)/shard_map/ppermute | solution.py:539
  23.3 2.1 %rows.1 = (f32[4,96,512]{2,1,0:T(8,128)S(1)}, bf16[256,512]{1,0:T(8,128)(2,1)S(1)}, f32[3,8,256]{2,1,0:T(8,128)S(1)}, f32[2,8,256]{2,1,0:T(8,128)S(1)}) custom-call(bf16[2,96,512]{2,1,0:T(8,128)(2,1)S(1)} %collective-permute-done.3.first_ref, bf16[2,96,512]{2,1,0:T(8,128)(2,1)S(1)} %collective-permute-done.2.second_ref, ...), custom_call_target="tpu_custom_call" | custom-call | flops 100000000 | bytes 1048576 | tf_op jit(solution)/shard_map/rows/pallas_call | solution.py:505
  25.5 0.6 %rims.1 = (bf16[208,512]{1,0:T(8,128)(2,1)S(1)}, bf16[208,512]{1,0:T(8,128)(2,1)S(1)}, bf16[208,512]{1,0:T(8,128)(2,1)S(1)}, bf16[208,512]{1,0:T(8,128)(2,1)S(1)}) custom-call(bf16[256,512]{1,0:T(8,128)(2,1)S(1)} %get-tuple-element.60.query_ref, bf16[256,512]{1,0:T(8,128)(2,1)S(1)} %get-tuple-element.59.dout_ref, ...), custom_call_target="tpu_custom_call" | custom-call | flops 100000000 | bytes 1048576 | tf_op jit(solution)/shard_map/rims/pallas_call | solution.py:505
  26.0 1.8 %collective-permute-start.7 = (bf16[208,512]{1,0:T(8,128)(2,1)S(1)}, bf16[208,512]{1,0:T(8,128)(2,1)S(1)}, u32[]{:S(2)}, u32[]{:S(2)}) collective-permute-start(bf16[208,512]{1,0:T(8,128)(2,1)S(1)} %get-tuple-element.84), channel_id=1, source_target_pairs={{0,24},{2,26},{4,28},{6,30},{8,16},{10,18},{12,20},{14,22},{16,8},... | collective-permute-start | bytes 638984 | tf_op jit(solution)/shard_map/ppermute | solution.py:539
  27.9 3.9 %collective-permute-done.5.arrived_ref = bf16[256,512]{1,0:T(8,128)(2,1)S(1)} collective-permute-done((bf16[256,512]{1,0:T(8,128)(2,1)S(1)}, bf16[256,512]{1,0:T(8,128)(2,1)S(1)}, u32[]{:S(2)}, u32[]{:S(2)}) %collective-permute-start.5) | collective-permute-done | bytes 262176 | tf_op jit(solution)/shard_map/ppermute | solution.py:525
  31.8 0.4 partial.1
  32.3 3.5 %collective-permute-start.9 = (bf16[208,512]{1,0:T(8,128)(2,1)S(1)}, bf16[208,512]{1,0:T(8,128)(2,1)S(1)}, u32[]{:S(2)}, u32[]{:S(2)}) collective-permute-start(bf16[208,512]{1,0:T(8,128)(2,1)S(1)} %get-tuple-element.87), channel_id=1, source_target_pairs={{0,30},{2,4},{4,2},{6,8},{8,6},{10,12},{12,10},{14,16},{16,14},{18... | collective-permute-start | bytes 638984 | tf_op jit(solution)/shard_map/ppermute | solution.py:539
  35.8 3.1 %backward.1 = (bf16[256,512]{1,0:T(8,128)(2,1)}, f32[2,256,512]{2,1,0:T(8,128)S(1)}) custom-call(bf16[2,96,512]{2,1,0:T(8,128)(2,1)S(1)} %collective-permute-done.second_ref.fourth_ref, bf16[2,96,512]{2,1,0:T(8,128)(2,1)S(1)} %collective-permute-done.1.first_ref.third_ref, bf16[2,96,512]{2,1,0:T(8,128)(2,1)S(1)} %collective-permute-done.2.second_ref, ...), custom_call_target="tpu_custom_call" | custom-call | flops 3000000000 | bytes 1048576 | tf_op jit(solution)/shard_map/backward/pallas_call | solution.py:505
  39.0 0.5 collective-permute-done.8.refs_5_.refs_4_
  39.4 1.0 %collective-permute-done.11.refs_1_ = bf16[4,64,512]{2,1,0:T(8,128)(2,1)S(1)} collective-permute-done((bf16[4,64,512]{2,1,0:T(8,128)(2,1)S(1)}, bf16[4,64,512]{2,1,0:T(8,128)(2,1)S(1)}, u32[]{:S(2)}, u32[]{:S(2)}) %collective-permute-start.11) | collective-permute-done | bytes 262176 | tf_op jit(solution)/shard_map/ppermute | solution.py:525
  40.5 2.9 %collective-permute-start.12 = (bf16[1,64,512]{2,1,0:T(8,128)(2,1)S(1)}, bf16[1,64,512]{2,1,0:T(8,128)(2,1)S(1)}, u32[]{:S(2)}, u32[]{:S(2)}) collective-permute-start(bf16[1,64,512]{2,1,0:T(8,128)(2,1)S(1)} %get-tuple-element.93), channel_id=1, source_target_pairs={{0,24},{2,26},{4,28},{6,30},{8,16},{10,18},{12,20},{14,22},{16,8},... | collective-permute-start | bytes 196616 | tf_op jit(solution)/shard_map/ppermute | solution.py:532
  43.4 1.0 %collective-permute-start.13 = (bf16[1,64,512]{2,1,0:T(8,128)(2,1)S(1)}, bf16[1,64,512]{2,1,0:T(8,128)(2,1)S(1)}, u32[]{:S(2)}, u32[]{:S(2)}) collective-permute-start(bf16[1,64,512]{2,1,0:T(8,128)(2,1)S(1)} %get-tuple-element.94), channel_id=1, source_target_pairs={{0,16},{2,18},{4,20},{6,22},{8,24},{10,26},{12,28},{14,30},{16,0},... | collective-permute-start | bytes 196616 | tf_op jit(solution)/shard_map/ppermute | solution.py:532
  44.4 0.5 %collective-permute-start.14 = (bf16[1,64,512]{2,1,0:T(8,128)(2,1)S(1)}, bf16[1,64,512]{2,1,0:T(8,128)(2,1)S(1)}, u32[]{:S(2)}, u32[]{:S(2)}) collective-permute-start(bf16[1,64,512]{2,1,0:T(8,128)(2,1)S(1)} %get-tuple-element.95), channel_id=1, source_target_pairs={{0,8},{2,10},{4,12},{6,14},{8,0},{10,2},{12,4},{14,6},{16,24},{18,... | collective-permute-start | bytes 196616 | tf_op jit(solution)/shard_map/ppermute | solution.py:532
  44.9 0.7 %collective-permute-done.10.refs_7_ = bf16[208,512]{1,0:T(8,128)(2,1)S(1)} collective-permute-done((bf16[208,512]{1,0:T(8,128)(2,1)S(1)}, bf16[208,512]{1,0:T(8,128)(2,1)S(1)}, u32[]{:S(2)}, u32[]{:S(2)}) %collective-permute-start.10) | collective-permute-done | bytes 213024 | tf_op jit(solution)/shard_map/ppermute | solution.py:539
  45.6 4.5 %sides.1 = (bf16[256,512]{1,0:T(8,128)(2,1)}, bf16[256,512]{1,0:T(8,128)(2,1)}) custom-call(f32[2,256,512]{2,1,0:T(8,128)S(1)} %get-tuple-element.82.centre_ref.refs_2_, bf16[256,512]{1,0:T(8,128)(2,1)S(1)} %get-tuple-element.83.chosen_ref, bf16[2,96,512]{2,1,0:T(8,128)(2,1)S(1)} %get-tuple-element.54.refs_0_, ...), custom_call_target="tpu_custom_call" | custom-call | flops 3000000000 | bytes 1048576 | tf_op jit(solution)/shard_map/sides/pallas_call | solution.py:505
  50.2 0.7 %weight_sum.1 = f32[64,512]{1,0:T(8,128)} custom-call(bf16[1,64,512]{2,1,0:T(8,128)(2,1)S(1)} %get-tuple-element.92.refs_0_, bf16[1,64,512]{2,1,0:T(8,128)(2,1)S(1)} %collective-permute-done.12.refs_1_, bf16[1,64,512]{2,1,0:T(8,128)(2,1)S(1)} %collective-permute-done.13.refs_2_, bf16[1,64,512]{2,1,0:T(8,128)(2,1)S(1)} %collective-permute-done.14.refs_3_), custom_call_target="tpu_custom_call" | custom-call | flops 100000000 | bytes 1048576 | tf_op jit(solution)/shard_map/weight_sum/pallas_call | solution.py:505
  (17 shorter events, 0.6 us)
Async XLA Ops:
  2.1 8.2 %collective-permute-start.4 = (bf16[256,512]{1,0:T(8,128)(2,1)}, bf16[256,512]{1,0:T(8,128)(2,1)S(1)}, u32[]{:S(2)}, u32[]{:S(2)}) collective-permute-start(bf16[256,512]{1,0:T(8,128)(2,1)} %refs_0_), channel_id=1, source_target_pairs={{1,0},{0,1},{3,2},{2,3},{5,4},{4,5},{7,6},{6,7},{9,8},{8,9},{11,10... | collective-permute-start | bytes 786440 | tf_op jit(solution)/shard_map/ppermute | solution.py:570
  2.7 15.3 %collective-permute-start = (bf16[2,96,512]{2,1,0:T(8,128)(2,1)S(1)}, bf16[2,96,512]{2,1,0:T(8,128)(2,1)S(1)}, u32[]{:S(2)}, u32[]{:S(2)}) collective-permute-start(bf16[2,96,512]{2,1,0:T(8,128)(2,1)S(1)} %get-tuple-element.54.refs_0_), channel_id=1, source_target_pairs={{0,24},{2,26},{4,28},{6,30},{8,16},{10,18},{12,20},{14,22},{16,8},... | collective-permute-start | bytes 589832 | tf_op jit(solution)/shard_map/ppermute | solution.py:539
  7.3 10.6 %collective-permute-start.1 = (bf16[2,96,512]{2,1,0:T(8,128)(2,1)S(1)}, bf16[2,96,512]{2,1,0:T(8,128)(2,1)S(1)}, u32[]{:S(2)}, u32[]{:S(2)}) collective-permute-start(bf16[2,96,512]{2,1,0:T(8,128)(2,1)S(1)} %get-tuple-element.55.refs_1_), channel_id=1, source_target_pairs={{0,8},{2,10},{4,12},{6,14},{8,0},{10,2},{12,4},{14,6},{16,24},{18,... | collective-permute-start | bytes 589832 | tf_op jit(solution)/shard_map/ppermute | solution.py:539
  7.3 16.0 %collective-permute-start.2 = (bf16[2,96,512]{2,1,0:T(8,128)(2,1)S(1)}, bf16[2,96,512]{2,1,0:T(8,128)(2,1)S(1)}, u32[]{:S(2)}, u32[]{:S(2)}) collective-permute-start(bf16[2,96,512]{2,1,0:T(8,128)(2,1)S(1)} %get-tuple-element.56.refs_2_), channel_id=1, source_target_pairs={{0,30},{2,4},{4,2},{6,8},{8,6},{10,12},{12,10},{14,16},{16,14},{18... | collective-permute-start | bytes 589832 | tf_op jit(solution)/shard_map/ppermute | solution.py:539
  10.1 13.2 %collective-permute-start.3 = (bf16[2,96,512]{2,1,0:T(8,128)(2,1)S(1)}, bf16[2,96,512]{2,1,0:T(8,128)(2,1)S(1)}, u32[]{:S(2)}, u32[]{:S(2)}) collective-permute-start(bf16[2,96,512]{2,1,0:T(8,128)(2,1)S(1)} %get-tuple-element.57.refs_3_), channel_id=1, source_target_pairs={{0,2},{2,0},{4,6},{6,4},{8,10},{10,8},{12,14},{14,12},{16,18},{18,... | collective-permute-start | bytes 589832 | tf_op jit(solution)/shard_map/ppermute | solution.py:539
  12.5 12.9 %collective-permute-start.6 = (bf16[2,4,64,256]{3,2,1,0:T(8,128)(2,1)S(1)}, bf16[2,4,64,256]{3,2,1,0:T(8,128)(2,1)S(1)}, u32[]{:S(2)}, u32[]{:S(2)}) collective-permute-start(bf16[2,4,64,256]{3,2,1,0:T(8,128)(2,1)S(1)} %get-tuple-element.77), channel_id=1, source_target_pairs={{0,2},{1,5},{2,0},{3,7},{4,6},{5,1},{6,4},{7,3},{8,10},{9,13},{10,... | collective-permute-start | bytes 786440 | tf_op jit(solution)/shard_map/ppermute | solution.py:525
  25.4 6.4 %collective-permute-start.5 = (bf16[256,512]{1,0:T(8,128)(2,1)S(1)}, bf16[256,512]{1,0:T(8,128)(2,1)S(1)}, u32[]{:S(2)}, u32[]{:S(2)}) collective-permute-start(bf16[256,512]{1,0:T(8,128)(2,1)S(1)} %get-tuple-element.75.attention_ref), channel_id=1, source_target_pairs={{0,2},{1,5},{2,0},{3,7},{4,6},{5,1},{6,4},{7,3},{8,10},{9,13},{10,... | collective-permute-start | bytes 786440 | tf_op jit(solution)/shard_map/ppermute | solution.py:525
  26.0 12.9 %collective-permute-start.7 = (bf16[208,512]{1,0:T(8,128)(2,1)S(1)}, bf16[208,512]{1,0:T(8,128)(2,1)S(1)}, u32[]{:S(2)}, u32[]{:S(2)}) collective-permute-start(bf16[208,512]{1,0:T(8,128)(2,1)S(1)} %get-tuple-element.84), channel_id=1, source_target_pairs={{0,24},{2,26},{4,28},{6,30},{8,16},{10,18},{12,20},{14,22},{16,8},... | collective-permute-start | bytes 638984 | tf_op jit(solution)/shard_map/ppermute | solution.py:539
  27.8 11.6 %collective-permute-start.8 = (bf16[208,512]{1,0:T(8,128)(2,1)S(1)}, bf16[208,512]{1,0:T(8,128)(2,1)S(1)}, u32[]{:S(2)}, u32[]{:S(2)}) collective-permute-start(bf16[208,512]{1,0:T(8,128)(2,1)S(1)} %get-tuple-element.85), channel_id=1, source_target_pairs={{0,8},{2,10},{4,12},{6,14},{8,0},{10,2},{12,4},{14,6},{16,24},{18,... | collective-permute-start | bytes 638984 | tf_op jit(solution)/shard_map/ppermute | solution.py:539
  32.3 8.2 %collective-permute-start.11 = (bf16[4,64,512]{2,1,0:T(8,128)(2,1)S(1)}, bf16[4,64,512]{2,1,0:T(8,128)(2,1)S(1)}, u32[]{:S(2)}, u32[]{:S(2)}) collective-permute-start(bf16[4,64,512]{2,1,0:T(8,128)(2,1)S(1)} %get-tuple-element.80.unused_ref), channel_id=1, source_target_pairs={{0,4},{1,3},{2,6},{3,1},{4,0},{5,7},{6,2},{7,5},{8,12},{9,11},{10,... | collective-permute-start | bytes 786440 | tf_op jit(solution)/shard_map/ppermute | solution.py:525
  32.3 12.6 %collective-permute-start.9 = (bf16[208,512]{1,0:T(8,128)(2,1)S(1)}, bf16[208,512]{1,0:T(8,128)(2,1)S(1)}, u32[]{:S(2)}, u32[]{:S(2)}) collective-permute-start(bf16[208,512]{1,0:T(8,128)(2,1)S(1)} %get-tuple-element.87), channel_id=1, source_target_pairs={{0,30},{2,4},{4,2},{6,8},{8,6},{10,12},{12,10},{14,16},{16,14},{18... | collective-permute-start | bytes 638984 | tf_op jit(solution)/shard_map/ppermute | solution.py:539
  35.8 9.8 %collective-permute-start.10 = (bf16[208,512]{1,0:T(8,128)(2,1)S(1)}, bf16[208,512]{1,0:T(8,128)(2,1)S(1)}, u32[]{:S(2)}, u32[]{:S(2)}) collective-permute-start(bf16[208,512]{1,0:T(8,128)(2,1)S(1)} %get-tuple-element.88.unused_ref), channel_id=1, source_target_pairs={{0,2},{2,0},{4,6},{6,4},{8,10},{10,8},{12,14},{14,12},{16,18},{18,... | collective-permute-start | bytes 638984 | tf_op jit(solution)/shard_map/ppermute | solution.py:539
  40.5 9.7 %collective-permute-start.12 = (bf16[1,64,512]{2,1,0:T(8,128)(2,1)S(1)}, bf16[1,64,512]{2,1,0:T(8,128)(2,1)S(1)}, u32[]{:S(2)}, u32[]{:S(2)}) collective-permute-start(bf16[1,64,512]{2,1,0:T(8,128)(2,1)S(1)} %get-tuple-element.93), channel_id=1, source_target_pairs={{0,24},{2,26},{4,28},{6,30},{8,16},{10,18},{12,20},{14,22},{16,8},... | collective-permute-start | bytes 196616 | tf_op jit(solution)/shard_map/ppermute | solution.py:532
  43.4 6.8 %collective-permute-start.13 = (bf16[1,64,512]{2,1,0:T(8,128)(2,1)S(1)}, bf16[1,64,512]{2,1,0:T(8,128)(2,1)S(1)}, u32[]{:S(2)}, u32[]{:S(2)}) collective-permute-start(bf16[1,64,512]{2,1,0:T(8,128)(2,1)S(1)} %get-tuple-element.94), channel_id=1, source_target_pairs={{0,16},{2,18},{4,20},{6,22},{8,24},{10,26},{12,28},{14,30},{16,0},... | collective-permute-start | bytes 196616 | tf_op jit(solution)/shard_map/ppermute | solution.py:532
  44.4 5.8 %collective-permute-start.14 = (bf16[1,64,512]{2,1,0:T(8,128)(2,1)S(1)}, bf16[1,64,512]{2,1,0:T(8,128)(2,1)S(1)}, u32[]{:S(2)}, u32[]{:S(2)}) collective-permute-start(bf16[1,64,512]{2,1,0:T(8,128)(2,1)S(1)} %get-tuple-element.95), channel_id=1, source_target_pairs={{0,8},{2,10},{4,12},{6,14},{8,0},{10,2},{12,4},{14,6},{16,24},{18,... | collective-permute-start | bytes 196616 | tf_op jit(solution)/shard_map/ppermute | solution.py:532
